TPU v7x, 32 devices: a whole 2x2x4 slice. The times are simulated.
32 devices in a mesh: fronts: 4 (over y, core), rows: 8 (over z, x).
Axes of the slice: x: 2, y: 2, z: 4, core: 2. Of those that a mesh axis runs over, the one named last changes fastest.
Arguments:
- lower_rhs: float32 [8, 8192, 512], P('fronts', 'rows'), may hold values from -6 to 6
- lower_vectors: float32 [8, 8192, 256], P('fronts', 'rows')
- lower_factors: float32 [8, 8, 256, 256], P('fronts', 'rows')
- merge_vectors: float32 [8, 8, 256, 256], P('fronts', 'rows')
- merge_factors: float32 [8, 8, 256, 256], P('fronts', 'rows')
- live_blocks: int32 [8], replicated, may hold values from 1 to 8, 32 in all
- parent_front: int32 [8, 1], replicated, may hold values from 0 to 3, as said below
- front_owner: int32 [4], replicated, may hold values from 0 to 3, as said below
- contrib_rows: int32 [8, 128], replicated, may hold values from 0 to 8191, as said below
- upper_rhs: float32 [4, 8192, 512], P('fronts', 'rows'), may hold values from -6 to 6
- upper_vectors: float32 [4, 8192, 256], P('fronts', 'rows')
- upper_factors: float32 [4, 8, 256, 256], P('fronts', 'rows')
- summit_vectors: float32 [4, 8, 256, 256], P('fronts', 'rows')
- summit_factors: float32 [4, 8, 256, 256], P('fronts', 'rows')
Outputs:
- lower_result: float32 [8, 8192, 512], P('fronts', 'rows')
- upper_result: float32 [4, 8192, 512], P('fronts', 'rows')
Inputs may be any that keep to these rules, and one draw needn't show every extreme that they name: `parent_front`: every parent front has between one and 4 children, and some parent has exactly 4. `front_owner`: each parent front has its own index of fronts. `contrib_rows`: row k of a child's contribution lands in its parent's row block k // 16; no two entries are equal.
All inputs are finite; a program needn't handle non-finite values.
Results may differ from a plain program's by a relative error of at most 0.0003.
Values sent between devices are 32-bit elements; how exact they have to be, the bound alone decides.
A program may use at most 128 MiB of HBM per device.

v0:
```python
import jax
import jax.numpy as jnp
from jax import lax
from jax.sharding import PartitionSpec as P

NPIV = 128


EXACT = lax.Precision.HIGHEST


def partner(value, axis, bit):
    mask = 2**bit
    pairs = [(source, source ^ mask) for source in range(lax.axis_size(axis))]
    return lax.ppermute(value, axis, pairs)


def from_root(value, axis, source):
    kept = jnp.where(lax.axis_index(axis) == source, value, 0).astype(value.dtype)
    return lax.psum(kept, axis)


def wy_apply(values, vectors, factors):
    project = jnp.einsum("fri,frn->fin", vectors, values, precision=EXACT)
    scaled = jnp.einsum("fij,fin->fjn", factors, project, precision=EXACT)
    return values - jnp.einsum("fri,fin->frn", vectors, scaled, precision=EXACT)


def combine(lead, rest, vectors, factors):
    inner = lead + jnp.einsum("fij,fin->fjn", vectors, rest, precision=EXACT)
    weight = jnp.einsum("fij,fin->fjn", factors, inner, precision=EXACT)
    return (lead - weight, rest - jnp.einsum("fij,fjn->fin", vectors, weight, precision=EXACT))


def run_tree(tops, vectors, factors, live, place):
    levels = lax.axis_size("rows").bit_length() - 1
    for level in range(levels):
        step = 1 << level
        leads = (place % (2 * step) == 0) & (place + step < live)
        follows = (place % (2 * step) == step) & (place < live)
        lead_side = leads[:, None, None]
        follow_side = follows[:, None, None]
        half = tops.shape[-1] // 2
        is_lead = place % (2 * step) == 0
        first_half = tops[..., :half]
        second_half = tops[..., half:]
        kept = jnp.where(is_lead, first_half, second_half)
        outgoing = jnp.where(is_lead, second_half, first_half)
        other, other_vectors, other_factors = partner((outgoing, vectors, factors), "rows", level)
        lead_part = jnp.where(is_lead, kept, other)
        rest_part = jnp.where(is_lead, other, kept)
        node_vectors = jnp.where(is_lead, other_vectors, vectors)
        node_factors = jnp.where(is_lead, other_factors, factors)
        lead_new, rest_new = combine(lead_part, rest_part, node_vectors, node_factors)
        returned = partner(jnp.where(is_lead, rest_new, lead_new), "rows", level)
        lead_whole = jnp.concatenate([lead_new, returned], axis=2)
        rest_whole = jnp.concatenate([returned, rest_new], axis=2)
        tops = jnp.where(lead_side, lead_whole, jnp.where(follow_side, rest_whole, tops))
    return tops


def per_device(
    lower_rhs,
    lower_vectors,
    lower_factors,
    merge_vectors,
    merge_factors,
    live_blocks,
    parent_front,
    front_owner,
    contrib_rows,
    upper_rhs,
    upper_vectors,
    upper_factors,
    summit_vectors,
    summit_factors,
):
    place = lax.axis_index("rows")
    column = lax.axis_index("fronts")
    blocks = lax.axis_size("rows")
    local_fronts = lower_rhs.shape[0]
    height = lower_rhs.shape[1]
    width = lower_factors.shape[-1]
    live = lax.dynamic_slice_in_dim(live_blocks, column * local_fronts, local_fronts)
    applied = wy_apply(lower_rhs, lower_vectors, lower_factors[:, 0])
    applied = jnp.where((place < live)[:, None, None], applied, lower_rhs)
    tops = run_tree(applied[:, :width], merge_vectors[:, 0], merge_factors[:, 0], live, place)
    keep = (jnp.arange(width) < NPIV)[None, :, None] | (place != 0)
    lower_result = jnp.concatenate([jnp.where(keep, tops, 0.0), applied[:, width:]], axis=1)
    contrib = tops[:, NPIV:]
    share = (width - NPIV) // blocks
    shared = from_root(contrib, "rows", 0)
    gathered = lax.all_gather(shared, "fronts", axis=0, tiled=True)
    front_portions = lax.dynamic_slice_in_dim(gathered, place * share, share, 1)
    parents = jnp.arange(front_owner.shape[0], dtype=jnp.int32)
    target = jnp.sum(jnp.where(parent_front == parents[None, :], front_owner[None, :], 0), axis=1)
    rows_here = lax.dynamic_slice_in_dim(contrib_rows, place * share, share, 1) - place * height
    rows_here = jnp.where((target == column)[:, None], rows_here, -1).reshape(-1)
    selector = (
        lax.broadcasted_iota(jnp.int32, (height, rows_here.shape[0]), 0) == rows_here[None, :]
    ).astype(jnp.float32)
    positioned_rows = jnp.dot(
        selector,
        front_portions.reshape(-1, front_portions.shape[-1]),
        precision=EXACT,
        preferred_element_type=jnp.float32,
    )
    taken = jnp.max(selector, axis=1) > 0
    assembled = jnp.where(taken[:, None], positioned_rows, upper_rhs[0])[None]
    upper_applied = wy_apply(assembled, upper_vectors, upper_factors[:, 0])
    whole = jnp.full((1,), blocks, jnp.int32)
    upper_tops = run_tree(
        upper_applied[:, :width], summit_vectors[:, 0], summit_factors[:, 0], whole, place
    )
    upper_result = jnp.concatenate([upper_tops, upper_applied[:, width:]], axis=1)
    return (lower_result, upper_result)


def solution(mesh):
    placed = (
        P("fronts", "rows", None),
        P("fronts", "rows", None),
        P("fronts", "rows", None, None),
        P("fronts", "rows", None, None),
        P("fronts", "rows", None, None),
        P(),
        P(),
        P(),
        P(),
        P("fronts", "rows", None),
        P("fronts", "rows", None),
        P("fronts", "rows", None, None),
        P("fronts", "rows", None, None),
        P("fronts", "rows", None, None),
    )
    return jax.shard_map(
        per_device,
        mesh=mesh,
        in_specs=placed,
        out_specs=(P("fronts", "rows", None), P("fronts", "rows", None)),
        check_vma=False,
    )
```

profile of v0, /device:TPU:0, one launch (start us, length us, event | category | flops | bytes accessed | tf_op | source)
XLA Modules:
  0.0 423.6 jit_solution(14652087842025641350)
XLA Ops:
  7.3 5.5 %copy.82 = f32[2,1024,512]{1,2,0:T(8,128)} copy(f32[2,1024,512]{2,1,0:T(8,128)} %param.14) | data formatting | bytes 8388608 | tf_op args[0]
  12.8 8.5 %fusion.74 = f32[2,256,512]{1,2,0:T(8,128)S(1)} fusion(f32[2,1024,256]{2,1,0:T(8,128)S(1)} %copy-done, f32[2,1024,512]{2,1,0:T(8,128)} %param.14), kind=kOutput, calls=%fused_computation.155 | convolution fusion | flops 3221225472 | bytes 7340032 | tf_op jit(solution)/shard_map/fri,frn->fin/dot_general | solution.py:24
  21.3 2.1 fusion.15
  23.5 5.8 %subtract_select_fusion = f32[2,1024,512]{1,2,0:T(8,128)S(1)} fusion(f32[2,1024,512]{1,2,0:T(8,128)} %copy.82, f32[2,512,256]{2,1,0:T(8,128)S(1)} %fusion.15, f32[2,1024,256]{2,1,0:T(8,128)S(1)} %copy-done, pred[2]{0:T(512)(128)(4,1)S(1)} %get-tuple-element.31), kind=kOutput, calls=%fused_computation | convolution fusion | flops 3223322624 | bytes 11534338 | tf_op jit(solution)/shard_map/fri,fin->frn/dot_general | solution.py:26
  29.4 2.0 copy-done.2
  32.3 2.9 collective-permute-start
  35.7 2.1 collective-permute-start.1
  37.8 10.4 %collective-permute-done = f32[2,256,256]{1,2,0:T(8,128)S(1)} collective-permute-done((f32[2,256,256]{1,2,0:T(8,128)}, f32[2,256,256]{1,2,0:T(8,128)S(1)}, u32[]{:S(2)}, u32[]{:S(2)}) %collective-permute-start) | collective-permute-done | bytes 524320 | tf_op jit(solution)/shard_map/ppermute | solution.py:15
  48.2 11.2 %collective-permute-done.2 = f32[2,256,256]{1,2,0:T(8,128)S(1)} collective-permute-done((f32[2,256,256]{1,2,0:T(8,128)S(1)}, f32[2,256,256]{1,2,0:T(8,128)S(1)}, u32[]{:S(2)}, u32[]{:S(2)}) %collective-permute-start.2) | collective-permute-done | bytes 524320 | tf_op jit(solution)/shard_map/ppermute | solution.py:15
  59.4 2.6 convolution_add_fusion.2
  62.1 7.8 %collective-permute-done.1 = f32[2,256,256]{1,2,0:T(8,128)S(1)} collective-permute-done((f32[2,256,256]{1,2,0:T(8,128)S(1)}, f32[2,256,256]{1,2,0:T(8,128)S(1)}, u32[]{:S(2)}, u32[]{:S(2)}) %collective-permute-start.1) | collective-permute-done | bytes 524320 | tf_op jit(solution)/shard_map/ppermute | solution.py:15
  70.9 2.8 broadcast_select_fusion.1
  73.6 1.7 collective-permute-start.3
  75.4 1.6 collective-permute-start.6
  77.0 10.0 %collective-permute-done.3 = f32[2,256,256]{1,2,0:T(8,128)S(1)} collective-permute-done((f32[2,256,256]{1,2,0:T(8,128)}, f32[2,256,256]{1,2,0:T(8,128)S(1)}, u32[]{:S(2)}, u32[]{:S(2)}) %collective-permute-start.3) | collective-permute-done | bytes 524320 | tf_op jit(solution)/shard_map/ppermute | solution.py:15
  87.0 1.5 fusion.10
  88.5 1.6 collective-permute-start.4
  90.6 12.8 %collective-permute-done.4 = f32[2,256,256]{1,2,0:T(8,128)S(1)} collective-permute-done((f32[2,256,256]{1,2,0:T(8,128)S(1)}, f32[2,256,256]{1,2,0:T(8,128)S(1)}, u32[]{:S(2)}, u32[]{:S(2)}) %collective-permute-start.4) | collective-permute-done | bytes 524320 | tf_op jit(solution)/shard_map/ppermute | solution.py:15
  104.2 7.8 %collective-permute-done.5 = f32[2,256,256]{1,2,0:T(8,128)S(1)} collective-permute-done((f32[2,256,256]{1,2,0:T(8,128)S(1)}, f32[2,256,256]{1,2,0:T(8,128)S(1)}, u32[]{:S(2)}, u32[]{:S(2)}) %collective-permute-start.5) | collective-permute-done | bytes 524320 | tf_op jit(solution)/shard_map/ppermute | solution.py:15
  113.5 1.3 collective-permute-start.7
  114.8 2.6 collective-permute-start.10
  117.4 18.6 %collective-permute-done.7 = f32[2,256,256]{1,2,0:T(8,128)S(1)} collective-permute-done((f32[2,256,256]{1,2,0:T(8,128)S(1)}, f32[2,256,256]{1,2,0:T(8,128)S(1)}, u32[]{:S(2)}, u32[]{:S(2)}) %collective-permute-start.7) | collective-permute-done | bytes 524320 | tf_op jit(solution)/shard_map/ppermute | solution.py:15
  136.4 2.9 collective-permute-start.9
  139.3 32.3 %collective-permute-done.8 = f32[2,256,256]{1,2,0:T(8,128)S(1)} collective-permute-done((f32[2,256,256]{1,2,0:T(8,128)S(1)}, f32[2,256,256]{1,2,0:T(8,128)S(1)}, u32[]{:S(2)}, u32[]{:S(2)}) %collective-permute-start.8) | collective-permute-done | bytes 524320 | tf_op jit(solution)/shard_map/ppermute | solution.py:15
  172.4 10.4 %collective-permute-done.9 = f32[2,256,256]{1,2,0:T(8,128)S(1)} collective-permute-done((f32[2,256,256]{1,2,0:T(8,128)S(1)}, f32[2,256,256]{1,2,0:T(8,128)S(1)}, u32[]{:S(2)}, u32[]{:S(2)}) %collective-permute-start.9) | collective-permute-done | bytes 524320 | tf_op jit(solution)/shard_map/ppermute | solution.py:15
  184.4 25.2 %collective-permute-done.11 = f32[2,256,256]{1,2,0:T(8,128)S(1)} collective-permute-done((f32[2,256,256]{1,2,0:T(8,128)S(1)}, f32[2,256,256]{1,2,0:T(8,128)S(1)}, u32[]{:S(2)}, u32[]{:S(2)}) %collective-permute-start.11) | collective-permute-done | bytes 524320 | tf_op jit(solution)/shard_map/ppermute | solution.py:15
  209.6 1.3 broadcast_select_fusion
  211.9 71.6 %all-reduce.2.cloned.1.call-done = f32[2,128,512]{1,2,0:T(8,128)} async-done(((f32[2,128,512]{1,2,0:T(8,128)}), f32[2,128,512]{1,2,0:T(8,128)}) %all-reduce.2.cloned.1.call-update) | async-done | bytes 524304 | tf_op jit(solution)/shard_map/psum | solution.py:20
  283.4 2.0 copy.98
  285.6 1.0 collective-permute-start.14
  286.9 2.0 copy.99
  289.1 18.4 %all-gather.2.cloned.1.call-done = f32[8,128,512]{2,1,0:T(8,128)} async-done(((f32[2,128,512]{2,1,0:T(8,128)}), f32[8,128,512]{2,1,0:T(8,128)}) %all-gather.2.cloned.1.call-update) | async-done | bytes 2097168 | tf_op jit(solution)/shard_map/all_gather | solution.py:93
  308.5 2.7 bitcast_select_fusion
  311.2 1.8 fusion.12
  313.7 2.0 fusion
  315.7 1.3 copy-done.3
  317.7 1.5 collective-permute-start.12
  320.0 7.1 %collective-permute-done.12 = f32[1,256,256]{1,2,0:T(8,128)S(1)} collective-permute-done((f32[1,256,256]{1,2,0:T(8,128)}, f32[1,256,256]{1,2,0:T(8,128)S(1)}, u32[]{:S(2)}, u32[]{:S(2)}) %collective-permute-start.12) | collective-permute-done | bytes 262176 | tf_op jit(solution)/shard_map/ppermute | solution.py:15
  327.1 1.7 fusion.2
  328.8 3.2 collective-permute-done.13
  332.5 1.2 broadcast_select_fusion.22
  333.7 1.5 collective-permute-start.15
  335.1 1.5 collective-permute-start.18
  336.6 4.9 %collective-permute-done.15 = f32[1,256,256]{1,2,0:T(8,128)S(1)} collective-permute-done((f32[1,256,256]{1,2,0:T(8,128)}, f32[1,256,256]{1,2,0:T(8,128)S(1)}, u32[]{:S(2)}, u32[]{:S(2)}) %collective-permute-start.15) | collective-permute-done | bytes 262176 | tf_op jit(solution)/shard_map/ppermute | solution.py:15
  342.2 1.2 fusion.14
  343.5 1.6 collective-permute-start.16
  345.6 7.2 %collective-permute-done.16 = f32[1,256,256]{1,2,0:T(8,128)S(1)} collective-permute-done((f32[1,256,256]{1,2,0:T(8,128)S(1)}, f32[1,256,256]{1,2,0:T(8,128)S(1)}, u32[]{:S(2)}, u32[]{:S(2)}) %collective-permute-start.16) | collective-permute-done | bytes 262176 | tf_op jit(solution)/shard_map/ppermute | solution.py:15
  352.8 1.4 fusion.5
  354.2 1.8 collective-permute-done.17
  356.4 2.1 broadcast_select_fusion.26
  359.1 2.4 collective-permute-start.22
  361.5 8.6 %collective-permute-done.19 = f32[1,256,256]{1,2,0:T(8,128)S(1)} collective-permute-done((f32[1,256,256]{1,2,0:T(8,128)S(1)}, f32[1,256,256]{1,2,0:T(8,128)S(1)}, u32[]{:S(2)}, u32[]{:S(2)}) %collective-permute-start.19) | collective-permute-done | bytes 262176 | tf_op jit(solution)/shard_map/ppermute | solution.py:15
  370.8 1.3 maximum_select_fusion.4
  372.2 2.9 collective-permute-start.21
  375.1 13.9 %collective-permute-done.20 = f32[1,256,256]{1,2,0:T(8,128)S(1)} collective-permute-done((f32[1,256,256]{1,2,0:T(8,128)S(1)}, f32[1,256,256]{1,2,0:T(8,128)S(1)}, u32[]{:S(2)}, u32[]{:S(2)}) %collective-permute-start.20) | collective-permute-done | bytes 262176 | tf_op jit(solution)/shard_map/ppermute | solution.py:15
  389.0 1.4 fusion.8
  390.3 4.1 collective-permute-done.21
  394.9 2.1 broadcast_select_fusion.30
  397.0 3.7 slice.79
  400.8 4.8 %pad_maximum_fusion = f32[2,1024,512]{1,2,0:T(8,128)} fusion(f32[2,768,512]{1,2,0:T(8,128)} %slice.79, f32[2,256,512]{1,2,0:T(8,128)} %get-tuple-element.16), kind=kLoop, calls=%fused_computation.1 | loop fusion | flops 1048576 | bytes 8388608 | tf_op jit(solution)/shard_map/concatenate | solution.py:89
  405.5 5.4 %copy.105 = f32[2,1024,512]{2,1,0:T(8,128)} copy(f32[2,1024,512]{1,2,0:T(8,128)} %pad_maximum_fusion) | data formatting | bytes 8388608
  411.0 1.3 slice-done
  412.3 1.6 pad_maximum_fusion.1
  413.9 2.9 copy.106
  (97 shorter events, 16.7 us)
Async XLA Ops:
  7.2 5.6 %copy-start = (f32[2,1024,256]{2,1,0:T(8,128)S(1)}, f32[2,1024,256]{2,1,0:T(8,128)}, u32[]{:S(2)}) copy-start(f32[2,1024,256]{2,1,0:T(8,128)} %param.15) | copy-start | bytes 6291460
  7.2 276.3 %all-reduce.2.cloned.1.call-start = ((), (), s32[]{:S(2)}) async-start(), calls=%async_computation | async-start | bytes 1048576 | tf_op jit(solution)/shard_map/psum | solution.py:20
  21.3 2.1 copy-start.19
  23.5 11.7 %copy-start.11 = (f32[2,1,256,256]{3,2,1,0:T(8,128)S(1)}, f32[2,1,256,256]{3,2,1,0:T(8,128)}, u32[]{:S(2)}) copy-start(f32[2,1,256,256]{3,2,1,0:T(8,128)} %param.17) | copy-start | bytes 1572868
  29.4 2.0 copy-start.2
  31.4 4.1 copy-start.12
  32.3 15.9 %collective-permute-start = (f32[2,256,256]{1,2,0:T(8,128)}, f32[2,256,256]{1,2,0:T(8,128)S(1)}, u32[]{:S(2)}, u32[]{:S(2)}) collective-permute-start(f32[2,256,256]{1,2,0:T(8,128)} %slice_select_fusion.7), channel_id=1, source_target_pairs={{0,1},{1,0},{2,3},{3,2},{4,5},{5,4},{6,7},{7,6},{8,9},{9,8},{10,11... | collective-permute-start | bytes 1572872 | tf_op jit(solution)/shard_map/ppermute | solution.py:15
  35.4 24.0 %collective-permute-start.2 = (f32[2,256,256]{1,2,0:T(8,128)S(1)}, f32[2,256,256]{1,2,0:T(8,128)S(1)}, u32[]{:S(2)}, u32[]{:S(2)}) collective-permute-start(f32[2,256,256]{1,2,0:T(8,128)S(1)} %bitcast.216), channel_id=1, source_target_pairs={{0,1},{1,0},{2,3},{3,2},{4,5},{5,4},{6,7},{7,6},{8,9},{9,8},{10,11... | collective-permute-start | bytes 1572872 | tf_op jit(solution)/shard_map/ppermute | solution.py:15
  35.7 34.1 %collective-permute-start.1 = (f32[2,256,256]{1,2,0:T(8,128)S(1)}, f32[2,256,256]{1,2,0:T(8,128)S(1)}, u32[]{:S(2)}, u32[]{:S(2)}) collective-permute-start(f32[2,256,256]{1,2,0:T(8,128)S(1)} %bitcast.222), channel_id=1, source_target_pairs={{0,1},{1,0},{2,3},{3,2},{4,5},{5,4},{6,7},{7,6},{8,9},{9,8},{10,11... | collective-permute-start | bytes 1572872 | tf_op jit(solution)/shard_map/ppermute | solution.py:15
  59.4 2.6 copy-start.9
  69.8 1.0 copy-start.10
  73.6 13.3 %collective-permute-start.3 = (f32[2,256,256]{1,2,0:T(8,128)}, f32[2,256,256]{1,2,0:T(8,128)S(1)}, u32[]{:S(2)}, u32[]{:S(2)}) collective-permute-start(f32[2,256,256]{1,2,0:T(8,128)} %get-tuple-element.26), channel_id=1, source_target_pairs={{0,1},{1,0},{2,3},{3,2},{4,5},{5,4},{6,7},{7,6},{8,9},{9,8},{10,11... | collective-permute-start | bytes 1572872 | tf_op jit(solution)/shard_map/ppermute | solution.py:15
  75.4 15.2 %collective-permute-start.6 = (f32[2,256,256]{1,2,0:T(8,128)S(1)}, f32[2,256,256]{1,2,0:T(8,128)S(1)}, u32[]{:S(2)}, u32[]{:S(2)}) collective-permute-start(f32[2,256,256]{1,2,0:T(8,128)S(1)} %bitcast.217), channel_id=1, source_target_pairs={{0,2},{1,3},{2,0},{3,1},{4,6},{5,7},{6,4},{7,5},{8,10},{9,11},{10,... | collective-permute-start | bytes 1572872 | tf_op jit(solution)/shard_map/ppermute | solution.py:15
  88.5 14.9 %collective-permute-start.4 = (f32[2,256,256]{1,2,0:T(8,128)S(1)}, f32[2,256,256]{1,2,0:T(8,128)S(1)}, u32[]{:S(2)}, u32[]{:S(2)}) collective-permute-start(f32[2,256,256]{1,2,0:T(8,128)S(1)} %slice_select_fusion.5), channel_id=1, source_target_pairs={{0,2},{1,3},{2,0},{3,1},{4,6},{5,7},{6,4},{7,5},{8,10},{9,11},{10,... | collective-permute-start | bytes 1572872 | tf_op jit(solution)/shard_map/ppermute | solution.py:15
  90.1 21.9 %collective-permute-start.5 = (f32[2,256,256]{1,2,0:T(8,128)S(1)}, f32[2,256,256]{1,2,0:T(8,128)S(1)}, u32[]{:S(2)}, u32[]{:S(2)}) collective-permute-start(f32[2,256,256]{1,2,0:T(8,128)S(1)} %bitcast.223), channel_id=1, source_target_pairs={{0,2},{1,3},{2,0},{3,1},{4,6},{5,7},{6,4},{7,5},{8,10},{9,11},{10,... | collective-permute-start | bytes 1572872 | tf_op jit(solution)/shard_map/ppermute | solution.py:15
  113.5 22.4 %collective-permute-start.7 = (f32[2,256,256]{1,2,0:T(8,128)S(1)}, f32[2,256,256]{1,2,0:T(8,128)S(1)}, u32[]{:S(2)}, u32[]{:S(2)}) collective-permute-start(f32[2,256,256]{1,2,0:T(8,128)S(1)} %get-tuple-element.24), channel_id=1, source_target_pairs={{0,2},{1,3},{2,0},{3,1},{4,6},{5,7},{6,4},{7,5},{8,10},{9,11},{10,... | collective-permute-start | bytes 1572872 | tf_op jit(solution)/shard_map/ppermute | solution.py:15
  114.8 24.5 %collective-permute-start.10 = (f32[2,256,256]{1,2,0:T(8,128)S(1)}, f32[2,256,256]{1,2,0:T(8,128)S(1)}, u32[]{:S(2)}, u32[]{:S(2)}) collective-permute-start(f32[2,256,256]{1,2,0:T(8,128)S(1)} %bitcast.218), channel_id=1, source_target_pairs={{0,4},{1,5},{2,6},{3,7},{4,0},{5,1},{6,2},{7,3},{8,12},{9,13},{10,... | collective-permute-start | bytes 1572872 | tf_op jit(solution)/shard_map/ppermute | solution.py:15
  136.3 35.3 %collective-permute-start.8 = (f32[2,256,256]{1,2,0:T(8,128)S(1)}, f32[2,256,256]{1,2,0:T(8,128)S(1)}, u32[]{:S(2)}, u32[]{:S(2)}) collective-permute-start(f32[2,256,256]{1,2,0:T(8,128)S(1)} %slice_select_fusion.3), channel_id=1, source_target_pairs={{0,4},{1,5},{2,6},{3,7},{4,0},{5,1},{6,2},{7,3},{8,12},{9,13},{10,... | collective-permute-start | bytes 1572872 | tf_op jit(solution)/shard_map/ppermute | solution.py:15
  136.4 46.5 %collective-permute-start.9 = (f32[2,256,256]{1,2,0:T(8,128)S(1)}, f32[2,256,256]{1,2,0:T(8,128)S(1)}, u32[]{:S(2)}, u32[]{:S(2)}) collective-permute-start(f32[2,256,256]{1,2,0:T(8,128)S(1)} %bitcast.224), channel_id=1, source_target_pairs={{0,4},{1,5},{2,6},{3,7},{4,0},{5,1},{6,2},{7,3},{8,12},{9,13},{10,... | collective-permute-start | bytes 1572872 | tf_op jit(solution)/shard_map/ppermute | solution.py:15
  184.3 25.3 %collective-permute-start.11 = (f32[2,256,256]{1,2,0:T(8,128)S(1)}, f32[2,256,256]{1,2,0:T(8,128)S(1)}, u32[]{:S(2)}, u32[]{:S(2)}) collective-permute-start(f32[2,256,256]{1,2,0:T(8,128)S(1)} %get-tuple-element.22), channel_id=1, source_target_pairs={{0,4},{1,5},{2,6},{3,7},{4,0},{5,1},{6,2},{7,3},{8,12},{9,13},{10,... | collective-permute-start | bytes 1572872 | tf_op jit(solution)/shard_map/ppermute | solution.py:15
  211.0 74.5 %copy-start.16 = (f32[1,1,256,256]{3,2,1,0:T(8,128)S(1)}, f32[1,1,256,256]{3,2,1,0:T(8,128)}, u32[]{:S(2)}) copy-start(f32[1,1,256,256]{3,2,1,0:T(8,128)} %param.26) | copy-start | bytes 786436
  211.0 75.7 %copy-start.20 = (s32[4]{0:T(128)S(1)}, s32[4]{0:T(128)}, u32[]{:S(2)}) copy-start(s32[4]{0:T(128)} %param.21) | copy-start | bytes 52
  211.0 75.7 %copy-start.21 = (s32[8,1]{0,1:T(1,128)S(1)}, s32[8,1]{0,1:T(1,128)}, u32[]{:S(2)}) copy-start(s32[8,1]{0,1:T(1,128)} %param.20) | copy-start | bytes 100
  211.0 75.8 %copy-start.18 = (s32[8,128]{1,0:T(8,128)S(1)}, s32[8,128]{1,0:T(8,128)}, u32[]{:S(2)}) copy-start(s32[8,128]{1,0:T(8,128)} %param.22) | copy-start | bytes 12292
  211.0 75.9 %copy-start.8 = (f32[1,1024,512]{2,1,0:T(8,128)S(1)}, f32[1,1024,512]{2,1,0:T(8,128)}, u32[]{:S(2)}) copy-start(f32[1,1024,512]{2,1,0:T(8,128)} %param.23) | copy-start | bytes 6291460
  211.8 95.7 %all-gather.2.cloned.1.call-start = ((), (), s32[]{:S(2)}) async-start(), calls=%async_computation.1 | async-start | bytes 2621440 | tf_op jit(solution)/shard_map/all_gather | solution.py:93
  285.6 34.3 %collective-permute-start.14 = (f32[1,256,256]{1,2,0:T(8,128)S(1)}, f32[1,256,256]{1,2,0:T(8,128)S(1)}, u32[]{:S(2)}, u32[]{:S(2)}) collective-permute-start(f32[1,256,256]{1,2,0:T(8,128)S(1)} %bitcast.219), channel_id=1, source_target_pairs={{0,1},{1,0},{2,3},{3,2},{4,5},{5,4},{6,7},{7,6},{8,9},{9,8},{10,11... | collective-permute-start | bytes 786440 | tf_op jit(solution)/shard_map/ppermute | solution.py:15
  308.5 2.7 copy-start.5
  311.2 1.8 copy-start.13
  313.7 5.6 %copy-start.17 = (f32[1,1,256,256]{3,2,1,0:T(8,128)S(1)}, f32[1,1,256,256]{3,2,1,0:T(8,128)}, u32[]{:S(2)}) copy-start(f32[1,1,256,256]{3,2,1,0:T(8,128)} %param.27) | copy-start | bytes 786436
  315.7 1.3 copy-start.3
  317.7 14.7 %copy-start.4 = (f32[1,1024,512]{1,2,0:T(8,128)S(1)}, f32[1,1024,512]{1,2,0:T(8,128)}, u32[]{:S(2)}) copy-start(f32[1,1024,512]{1,2,0:T(8,128)} %copy-done.3) | copy-start | bytes 6291460
  317.7 9.4 %collective-permute-start.12 = (f32[1,256,256]{1,2,0:T(8,128)}, f32[1,256,256]{1,2,0:T(8,128)S(1)}, u32[]{:S(2)}, u32[]{:S(2)}) collective-permute-start(f32[1,256,256]{1,2,0:T(8,128)} %slice_select_fusion.13), channel_id=1, source_target_pairs={{0,1},{1,0},{2,3},{3,2},{4,5},{5,4},{6,7},{7,6},{8,9},{9,8},{10,11... | collective-permute-start | bytes 786440 | tf_op jit(solution)/shard_map/ppermute | solution.py:15
  319.3 36.6 %copy-start.6 = (f32[1,1,256,256]{2,3,1,0:T(8,128)}, f32[1,1,256,256]{2,3,1,0:T(8,128)S(1)}, u32[]{:S(2)}) copy-start(f32[1,1,256,256]{2,3,1,0:T(8,128)S(1)} %copy.100) | copy-start | bytes 786436
  319.4 12.7 %collective-permute-start.13 = (f32[1,256,256]{1,2,0:T(8,128)S(1)}, f32[1,256,256]{1,2,0:T(8,128)S(1)}, u32[]{:S(2)}, u32[]{:S(2)}) collective-permute-start(f32[1,256,256]{1,2,0:T(8,128)S(1)} %bitcast.225), channel_id=1, source_target_pairs={{0,1},{1,0},{2,3},{3,2},{4,5},{5,4},{6,7},{7,6},{8,9},{9,8},{10,11... | collective-permute-start | bytes 786440 | tf_op jit(solution)/shard_map/ppermute | solution.py:15
  333.7 7.8 %collective-permute-start.15 = (f32[1,256,256]{1,2,0:T(8,128)}, f32[1,256,256]{1,2,0:T(8,128)S(1)}, u32[]{:S(2)}, u32[]{:S(2)}) collective-permute-start(f32[1,256,256]{1,2,0:T(8,128)} %get-tuple-element.14), channel_id=1, source_target_pairs={{0,1},{1,0},{2,3},{3,2},{4,5},{5,4},{6,7},{7,6},{8,9},{9,8},{10,11... | collective-permute-start | bytes 786440 | tf_op jit(solution)/shard_map/ppermute | solution.py:15
  335.1 10.4 %collective-permute-start.18 = (f32[1,256,256]{1,2,0:T(8,128)S(1)}, f32[1,256,256]{1,2,0:T(8,128)}, u32[]{:S(2)}, u32[]{:S(2)}) collective-permute-start(f32[1,256,256]{1,2,0:T(8,128)S(1)} %bitcast.220), channel_id=1, source_target_pairs={{0,2},{1,3},{2,0},{3,1},{4,6},{5,7},{6,4},{7,5},{8,10},{9,11},{10,... | collective-permute-start | bytes 786440 | tf_op jit(solution)/shard_map/ppermute | solution.py:15
  341.5 0.7 copy-start.14
  343.5 9.3 %collective-permute-start.16 = (f32[1,256,256]{1,2,0:T(8,128)S(1)}, f32[1,256,256]{1,2,0:T(8,128)S(1)}, u32[]{:S(2)}, u32[]{:S(2)}) collective-permute-start(f32[1,256,256]{1,2,0:T(8,128)S(1)} %slice_select_fusion.11), channel_id=1, source_target_pairs={{0,2},{1,3},{2,0},{3,1},{4,6},{5,7},{6,4},{7,5},{8,10},{9,11},{10,... | collective-permute-start | bytes 786440 | tf_op jit(solution)/shard_map/ppermute | solution.py:15
  345.0 10.9 %collective-permute-start.17 = (f32[1,256,256]{1,2,0:T(8,128)S(1)}, f32[1,256,256]{1,2,0:T(8,128)S(1)}, u32[]{:S(2)}, u32[]{:S(2)}) collective-permute-start(f32[1,256,256]{1,2,0:T(8,128)S(1)} %bitcast.226), channel_id=1, source_target_pairs={{0,2},{1,3},{2,0},{3,1},{4,6},{5,7},{6,4},{7,5},{8,10},{9,11},{10,... | collective-permute-start | bytes 786440 | tf_op jit(solution)/shard_map/ppermute | solution.py:15
  358.5 11.5 %collective-permute-start.19 = (f32[1,256,256]{1,2,0:T(8,128)S(1)}, f32[1,256,256]{1,2,0:T(8,128)S(1)}, u32[]{:S(2)}, u32[]{:S(2)}) collective-permute-start(f32[1,256,256]{1,2,0:T(8,128)S(1)} %get-tuple-element.12), channel_id=1, source_target_pairs={{0,2},{1,3},{2,0},{3,1},{4,6},{5,7},{6,4},{7,5},{8,10},{9,11},{10,... | collective-permute-start | bytes 786440 | tf_op jit(solution)/shard_map/ppermute | solution.py:15
  359.1 16.0 %collective-permute-start.22 = (f32[1,256,256]{1,2,0:T(8,128)S(1)}, f32[1,256,256]{1,2,0:T(8,128)}, u32[]{:S(2)}, u32[]{:S(2)}) collective-permute-start(f32[1,256,256]{1,2,0:T(8,128)S(1)} %bitcast.221), channel_id=1, source_target_pairs={{0,4},{1,5},{2,6},{3,7},{4,0},{5,1},{6,2},{7,3},{8,12},{9,13},{10,... | collective-permute-start | bytes 786440 | tf_op jit(solution)/shard_map/ppermute | solution.py:15
  361.5 10.7 %copy-start.7 = (f32[1,1,256,256]{2,3,1,0:T(8,128)S(1)}, f32[1,1,256,256]{2,3,1,0:T(8,128)}, u32[]{:S(2)}) copy-start(f32[1,1,256,256]{2,3,1,0:T(8,128)} %copy-done.6) | copy-start | bytes 786436
  370.1 0.7 copy-start.15
  372.1 16.9 %collective-permute-start.20 = (f32[1,256,256]{1,2,0:T(8,128)S(1)}, f32[1,256,256]{1,2,0:T(8,128)S(1)}, u32[]{:S(2)}, u32[]{:S(2)}) collective-permute-start(f32[1,256,256]{1,2,0:T(8,128)S(1)} %slice_select_fusion.9), channel_id=1, source_target_pairs={{0,4},{1,5},{2,6},{3,7},{4,0},{5,1},{6,2},{7,3},{8,12},{9,13},{10,... | collective-permute-start | bytes 786440 | tf_op jit(solution)/shard_map/ppermute | solution.py:15
  372.2 22.3 %collective-permute-start.21 = (f32[1,256,256]{1,2,0:T(8,128)S(1)}, f32[1,256,256]{1,2,0:T(8,128)S(1)}, u32[]{:S(2)}, u32[]{:S(2)}) collective-permute-start(f32[1,256,256]{1,2,0:T(8,128)S(1)} %bitcast.227), channel_id=1, source_target_pairs={{0,4},{1,5},{2,6},{3,7},{4,0},{5,1},{6,2},{7,3},{8,12},{9,13},{10,... | collective-permute-start | bytes 786440 | tf_op jit(solution)/shard_map/ppermute | solution.py:15
  397.0 13.9 %collective-permute-start.23 = (f32[1,256,256]{1,2,0:T(8,128)}, f32[1,256,256]{1,2,0:T(8,128)S(1)}, u32[]{:S(2)}, u32[]{:S(2)}) collective-permute-start(f32[1,256,256]{1,2,0:T(8,128)} %get-tuple-element.10), channel_id=1, source_target_pairs={{0,4},{1,5},{2,6},{3,7},{4,0},{5,1},{6,2},{7,3},{8,12},{9,13},{10,... | collective-permute-start | bytes 786440 | tf_op jit(solution)/shard_map/ppermute | solution.py:15
  410.9 1.4 slice-start
  412.3 4.5 %copy-start.1 = (f32[2,1024,256]{2,1,0:T(8,128)S(1)}, f32[2,1024,256]{2,1,0:T(8,128)}, u32[]{:S(2)}) copy-start(f32[2,1024,256]{2,1,0:T(8,128)} %param.15) | copy-start | bytes 6291460
Sparse Core Ops, SparseCore 0:
  212.0 71.4 all-reduce.1
  285.6 21.8 all-gather.1
where the time goes:
time: 424 us
  waiting for transfers between devices  287 us (68%)
  matrix products  45.4 us (11%)
  starting transfers between devices  31.5 us (7%)
  local copies, waits for them, and re-layouts  29.7 us (7%)
  other arithmetic  15.1 us (4%)
  between operations  14.6 us (3%)
    ppermute x24, waiting for transfers between devices, partner(): return lax.ppermute(value, axis, pairs)  197 us
    psum x1, waiting for transfers between devices, from_root(): return lax.psum(kept, axis)  71.6 us
    ppermute x24, starting transfers between devices, partner(): return lax.ppermute(value, axis, pairs)  31.4 us
    unnamed x52, local copies, waits for them, and re-layouts  21.5 us
    all_gather x1, waiting for transfers between devices, per_device(): gathered = lax.all_gather(shared, 'fronts', axis=0, tiled=True)  18.4 us
    dot_general x2, matrix products, wy_apply(): project = jnp.einsum('fri,frn->fin', vectors, values, precision=EXACT)  10.3 us
    dot_general x6, matrix products, combine(): jnp.einsum('fij,fjn->fin', vectors, weight, precision=EXACT)  9.83 us
    dot_general x6, matrix products, combine(): inner = lead + jnp.einsum('fij,fin->fjn', vectors, rest, precision=EXACT)  8.69 us
  transfers between devices with their start and end apart: 26, of which 20 were waited for; matrix products, arithmetic and copies ran while one was open for 9% of the time, Pallas kernels for 0%

commit v1 on v0

v1 whole, which is shorter than its diff:
```python
import jax
import jax.numpy as jnp
from jax import lax
from jax.sharding import PartitionSpec as P

NPIV = 128


EXACT = lax.Precision.HIGHEST
NEAR = lax.Precision.HIGH


def moved(value, axis, pairs):
    return lax.ppermute(value, axis, pairs)


def product(form, left, right):
    return jnp.einsum(form, left, right, precision=NEAR)


def wy_apply(values, vectors, factors):
    project = product("ri,rn->in", vectors, values)
    scaled = product("ij,in->jn", factors, project)
    return values - product("ri,in->rn", vectors, scaled)


def node_pairs(axis, level):
    step = 1 << level
    return [(p, p - step) for p in range(step, lax.axis_size(axis), 2 * step)]


def lead_factors(factors, levels):
    return [moved(factors, "rows", node_pairs("rows", level)) for level in range(levels)]


def run_tree(top, vectors, leads, live, place):
    back = jnp.zeros_like(top)
    for level, factors in enumerate(leads):
        step = 1 << level
        up = node_pairs("rows", level)
        arrived = moved(product("ij,in->jn", vectors, top), "rows", up)
        weight = product("ij,in->jn", factors, top + arrived)
        active = (place % (2 * step) == 0) & (place + step < live)
        weight = jnp.where(active, weight, 0.0)
        top = top - weight
        back = back + moved(weight, "rows", [(q, p) for p, q in up])
    return top, back


def spread(contrib, place, blocks):
    piece = contrib
    step = blocks // 2
    while step:
        half = piece.shape[0] // 2
        got = moved(piece[half:], "rows", [(q, q + step) for q in range(0, blocks, 2 * step)])
        piece = jnp.where(place % (2 * step) == step, got, piece[:half])
        step //= 2
    return piece


def per_device(
    lower_rhs,
    lower_vectors,
    lower_factors,
    merge_vectors,
    merge_factors,
    live_blocks,
    parent_front,
    front_owner,
    contrib_rows,
    upper_rhs,
    upper_vectors,
    upper_factors,
    summit_vectors,
    summit_factors,
):
    place = lax.axis_index("rows")
    column = lax.axis_index("fronts")
    blocks = lax.axis_size("rows")
    local_fronts = lower_rhs.shape[0]
    height = lower_rhs.shape[1]
    width = lower_factors.shape[-1]
    live = lax.dynamic_slice_in_dim(live_blocks, column * local_fronts, local_fronts)
    levels = blocks.bit_length() - 1
    share = (width - NPIV) // blocks
    leads = [lead_factors(merge_factors[f, 0], levels) for f in range(local_fronts)]
    summit_leads = lead_factors(summit_factors[0, 0], levels)
    applied, trees, portions = [], [], []
    for f in range(local_fronts):
        done = wy_apply(lower_rhs[f], lower_vectors[f], lower_factors[f, 0])
        applied.append(jnp.where(place < live[f], done, lower_rhs[f]))
    for f in range(local_fronts):
        trees.append(
            run_tree(applied[f][:width], merge_vectors[f, 0], leads[f], live[f], place)
        )
        portions.append(spread(trees[f][0][NPIV:], place, blocks))
    mine = jnp.stack(portions)
    columns = lax.axis_size("fronts")
    gathered = jnp.zeros((columns,) + mine.shape, mine.dtype)
    gathered = lax.dynamic_update_slice_in_dim(gathered, mine[None], column, 0)
    for shift in range(1, columns):
        got = moved(mine, "fronts", [(c, (c + shift) % columns) for c in range(columns)])
        gathered = lax.dynamic_update_slice_in_dim(
            gathered, got[None], (column - shift) % columns, 0
        )
    front_portions = gathered.reshape(-1, share, gathered.shape[-1])
    parents = jnp.arange(front_owner.shape[0], dtype=jnp.int32)
    target = jnp.sum(jnp.where(parent_front == parents[None, :], front_owner[None, :], 0), axis=1)
    rows_here = lax.dynamic_slice_in_dim(contrib_rows, place * share, share, 1) - place * height
    rows_here = jnp.where((target == column)[:, None], rows_here, -1).reshape(-1)
    selector = (
        lax.broadcasted_iota(jnp.int32, (height, rows_here.shape[0]), 0) == rows_here[None, :]
    ).astype(jnp.float32)
    positioned_rows = jnp.dot(
        selector,
        front_portions.reshape(-1, front_portions.shape[-1]),
        precision=EXACT,
        preferred_element_type=jnp.float32,
    )
    taken = jnp.max(selector, axis=1) > 0
    assembled = jnp.where(taken[:, None], positioned_rows, upper_rhs[0])
    upper_applied = wy_apply(assembled, upper_vectors[0], upper_factors[0, 0])
    upper_top, upper_back = run_tree(
        upper_applied[:width], summit_vectors[0, 0], summit_leads, blocks, place
    )
    upper_top = upper_top - product("ij,jn->in", summit_vectors[0, 0], upper_back)
    upper_result = lax.dynamic_update_slice(upper_applied, upper_top, (0, 0))[None]
    keep = (jnp.arange(width) < NPIV)[:, None] | (place != 0)
    lower = []
    for f in range(local_fronts):
        top, back = trees[f]
        top = top - product("ij,jn->in", merge_vectors[f, 0], back)
        lower.append(lax.dynamic_update_slice(applied[f], jnp.where(keep, top, 0.0), (0, 0)))
    return (jnp.stack(lower), upper_result)


def solution(mesh):
    placed = (
        P("fronts", "rows", None),
        P("fronts", "rows", None),
        P("fronts", "rows", None, None),
        P("fronts", "rows", None, None),
        P("fronts", "rows", None, None),
        P(),
        P(),
        P(),
        P(),
        P("fronts", "rows", None),
        P("fronts", "rows", None),
        P("fronts", "rows", None, None),
        P("fronts", "rows", None, None),
        P("fronts", "rows", None, None),
    )
    return jax.shard_map(
        per_device,
        mesh=mesh,
        in_specs=placed,
        out_specs=(P("fronts", "rows", None), P("fronts", "rows", None)),
        check_vma=False,
    )
```

time: 424 us -> 302 us (0.71)
  waiting for transfers between devices: 287 us -> 135 us
  starting transfers between devices: 31.5 us -> 63.7 us
  matrix products: 45.4 us -> 60.2 us
  other arithmetic: 15.1 us -> 4.39 us
  between operations: 14.6 us -> 6.56 us
    psum x1 -> x0, waiting for transfers between devices: 71.6 us -> none  [from_root(): return lax.psum(kept, axis)]
    ppermute x24 -> x36, waiting for transfers between devices: 197 us -> 135 us  [moved(): return lax.ppermute(value, axis, pairs)]
    ppermute x24 -> x36, starting transfers between devices: 31.4 us -> 63.7 us  [moved(): return lax.ppermute(value, axis, pairs)]
    all_gather x1 -> x0, waiting for transfers between devices: 18.4 us -> none  [per_device(): gathered = lax.all_gather(shared, 'fronts', axis=0, tiled=True)]
    dot_general x24 -> x30, matrix products: 42.7 us -> 57.5 us  [product(): return jnp.einsum(form, left, right, precision=NEAR)]
    select_n x13 -> x4, other arithmetic: 8.34 us -> 0.12 us  [spread(): piece = jnp.where(place % (2 * step) == step, got, piece[:half])]
    concatenate x2 -> x0, other arithmetic: 6.37 us -> none  [the longest x1 4.77 us: per_device(): jnp.concatenate([jnp.where(keep, tops, 0.0), applied[:, width:]], axis=1)]
    unnamed x52 -> x59, local copies, waits for them, and re-layouts: 21.5 us -> 19.2 us
  transfers between devices with their start and end apart: 26 -> 36, of which waited for: 20 -> 19; matrix products, arithmetic and copies ran while one was open for 9% -> 25% of each run, Pallas kernels for 0% -> 0%
where the time goes in v1:
time: 302 us; the launch traced here: 300 us
  waiting for transfers between devices  135 us (45%)
  starting transfers between devices  63.7 us (21%)
  matrix products  60.2 us (20%)
  local copies, waits for them, and re-layouts  30.3 us (10%)
  between operations  6.56 us (2%)
  other arithmetic  4.39 us (1%)
    ppermute x36, waiting for transfers between devices, moved(): return lax.ppermute(value, axis, pairs)  135 us
    ppermute x36, starting transfers between devices, moved(): return lax.ppermute(value, axis, pairs)  63.7 us
    dot_general x30, matrix products, product(): return jnp.einsum(form, left, right, precision=NEAR)  57.5 us
    unnamed x59, local copies, waits for them, and re-layouts  19.2 us
  transfers between devices with their start and end apart: 36, of which 19 were waited for; matrix products, arithmetic and copies ran while one was open for 25% of the time, Pallas kernels for 0%

profile of v1, /device:TPU:0, one launch (start us, length us, event | category | flops | bytes accessed | tf_op | source)
XLA Modules:
  0.0 300.3 jit_solution(16131154465690796471)
XLA Ops:
  0.6 1.9 slice_bitcast_fusion.1
  6.5 4.7 %fusion.93 = (f32[1,1024,512]{2,1,0:T(8,128)}, f32[1,1024,512]{2,1,0:T(8,128)}) fusion(f32[2,1024,512]{2,1,0:T(8,128)} %param.14), kind=kLoop, calls=%fused_computation.140 | loop fusion | bytes 8388608 | tf_op jit(solution)/shard_map/slice | solution.py:90
  11.2 3.1 %copy.80 = f32[1,1024,512]{1,2,0:T(8,128)} copy(f32[1,1024,512]{2,1,0:T(8,128)} %get-tuple-element.11) | data formatting | bytes 4194304
  14.2 3.4 %fusion = f32[256,512]{1,0:T(8,128)} fusion(f32[2,1024,256]{2,1,0:T(8,128)S(1)} %copy-done.9, f32[2,1024,512]{2,1,0:T(8,128)} %param.14), kind=kOutput, calls=%fused_computation.3 | convolution fusion | flops 805306368 | bytes 3670016 | tf_op jit(solution)/shard_map/ri,rn->in/dot_general | solution.py:18
  18.4 2.5 fusion.69
  21.6 3.3 %subtract_select_fusion = f32[1024,512]{0,1:T(8,128)S(1)} fusion(f32[1,1024,512]{1,2,0:T(8,128)} %copy.80, f32[512,256]{1,0:T(8,128)} %fusion.69, pred[]{:T(512)S(6)} %lt.121, f32[2,1024,256]{2,1,0:T(8,128)} %param.15), kind=kOutput, calls=%fused_computation.1 | convolution fusion | flops 806354944 | bytes 5767169 | tf_op jit(solution)/shard_map/ri,in->rn/dot_general | solution.py:18
  28.7 1.9 fusion.2
  30.6 2.9 copy.79
  33.5 2.5 fusion.75
  36.7 4.5 %subtract_select_fusion.1 = f32[1024,512]{0,1:T(8,128)} fusion(f32[1,1024,512]{1,2,0:T(8,128)} %copy.79, f32[512,256]{1,0:T(8,128)} %fusion.75, pred[]{:T(512)S(6)} %lt.112, f32[2,1024,256]{2,1,0:T(8,128)} %param.15), kind=kOutput, calls=%fused_computation.2 | convolution fusion | flops 806354944 | bytes 5767169 | tf_op jit(solution)/shard_map/ri,in->rn/dot_general | solution.py:18
  43.9 1.6 convolution_bitcast_fusion.11
  45.5 1.4 collective-permute-start.3
  48.3 1.5 fusion.9
  51.5 12.6 %collective-permute-done = f32[256,512]{0,1:T(8,128)S(1)} collective-permute-done((f32[256,512]{0,1:T(8,128)S(1)}, f32[256,512]{0,1:T(8,128)S(1)}, u32[]{:S(2)}, u32[]{:S(2)}) %collective-permute-start) | collective-permute-done | bytes 524320 | tf_op jit(solution)/shard_map/ppermute | solution.py:14
  65.4 2.1 fusion.12
  67.6 1.4 convolution_bitcast_fusion.10
  70.3 10.6 %collective-permute-done.11 = f32[256,512]{0,1:T(8,128)S(1)} collective-permute-done((f32[256,512]{0,1:T(8,128)S(1)}, f32[256,512]{0,1:T(8,128)S(1)}, u32[]{:S(2)}, u32[]{:S(2)}) %collective-permute-start.11) | collective-permute-done | bytes 524320 | tf_op jit(solution)/shard_map/ppermute | solution.py:14
  80.9 2.1 fusion.89
  85.5 16.1 %collective-permute-done.2 = f32[256,512]{0,1:T(8,128)S(1)} collective-permute-done((f32[256,512]{0,1:T(8,128)S(1)}, f32[256,512]{0,1:T(8,128)S(1)}, u32[]{:S(2)}, u32[]{:S(2)}) %collective-permute-start.2) | collective-permute-done | bytes 524320 | tf_op jit(solution)/shard_map/ppermute | solution.py:14
  101.6 2.4 fusion.88
  105.2 1.5 collective-permute-start.4
  108.2 2.9 copy.68
  111.1 2.6 fusion.95
  113.8 6.1 %collective-permute-start.21 = (f32[64,512]{0,1:T(8,128)S(1)}, f32[64,512]{0,1:T(8,128)S(1)}, u32[]{:S(2)}, u32[]{:S(2)}) collective-permute-start(f32[64,512]{0,1:T(8,128)S(1)} %slice.128), channel_id=1, source_target_pairs={{0,4},{8,12},{16,20},{24,28}} | collective-permute-start | bytes 393224 | tf_op jit(solution)/shard_map/ppermute | solution.py:14
  120.5 2.3 fusion.96
  122.9 1.5 collective-permute-start.18
  126.9 4.2 %collective-permute-done.18 = f32[64,512]{0,1:T(8,128)S(1)} collective-permute-done((f32[64,512]{0,1:T(8,128)S(1)}, f32[64,512]{0,1:T(8,128)S(1)}, u32[]{:S(2)}, u32[]{:S(2)}) %collective-permute-start.18) | collective-permute-done | bytes 131104 | tf_op jit(solution)/shard_map/ppermute | solution.py:14
  131.3 1.3 collective-permute-start.19
  132.6 4.1 %collective-permute-done.22 = f32[32,512]{0,1:T(8,128)S(1)} collective-permute-done((f32[32,512]{0,1:T(8,128)S(1)}, f32[32,512]{0,1:T(8,128)S(1)}, u32[]{:S(2)}, u32[]{:S(2)}) %collective-permute-start.22) | collective-permute-done | bytes 65568 | tf_op jit(solution)/shard_map/ppermute | solution.py:14
  136.9 1.3 collective-permute-start.23
  138.2 2.4 collective-permute-done.19
  141.5 2.0 collective-permute-start.20
  145.3 2.5 collective-permute-done.20
  149.7 2.6 collective-permute-start.25
  152.3 1.4 collective-permute-start.26
  155.6 2.7 bitcast_select_fusion
  160.8 1.3 copy-done.3
  165.9 20.7 %collective-permute-done.28 = f32[256,256]{1,0:T(8,128)} collective-permute-done((f32[256,256]{1,0:T(8,128)}, f32[256,256]{1,0:T(8,128)}, u32[]{:S(2)}, u32[]{:S(2)}) %collective-permute-start.28) | collective-permute-done | bytes 262176 | tf_op jit(solution)/shard_map/ppermute | solution.py:14
  186.6 1.6 fusion.6
  189.1 2.2 convolution_bitcast_fusion.2
  193.9 2.5 collective-permute-start.15
  196.4 16.7 %collective-permute-done.30 = f32[256,256]{1,0:T(8,128)} collective-permute-done((f32[256,256]{1,0:T(8,128)}, f32[256,256]{1,0:T(8,128)}, u32[]{:S(2)}, u32[]{:S(2)}) %collective-permute-start.30) | collective-permute-done | bytes 262176 | tf_op jit(solution)/shard_map/ppermute | solution.py:14
  213.1 3.0 fusion.90
  220.6 2.1 collective-permute-start.6
  222.7 2.5 collective-permute-start.16
  225.3 14.6 %collective-permute-done.32 = f32[256,256]{1,0:T(8,128)} collective-permute-done((f32[256,256]{1,0:T(8,128)}, f32[256,256]{1,0:T(8,128)}, u32[]{:S(2)}, u32[]{:S(2)}) %collective-permute-start.32) | collective-permute-done | bytes 262176 | tf_op jit(solution)/shard_map/ppermute | solution.py:14
  239.8 2.2 collective-permute-start.17
  242.1 1.5 collective-permute-start.7
  243.6 1.6 collective-permute-start.8
  245.2 2.4 fusion.4
  247.6 2.1 collective-permute-start.33
  249.7 2.1 collective-permute-start.34
  251.9 2.1 collective-permute-done.17
  254.0 6.1 %collective-permute-start.35 = (f32[256,512]{0,1:T(8,128)}, f32[256,512]{0,1:T(8,128)}, u32[]{:S(2)}, u32[]{:S(2)}) collective-permute-start(f32[256,512]{0,1:T(8,128)} %fusion.4), channel_id=1, source_target_pairs={{0,4},{8,12},{16,20},{24,28}} | collective-permute-start | bytes 1572872 | tf_op jit(solution)/shard_map/ppermute | solution.py:14
  260.0 1.8 fusion.20
  261.9 3.3 %collective-permute-done.7 = f32[256,512]{0,1:T(8,128)S(1)} collective-permute-done((f32[256,512]{0,1:T(8,128)}, f32[256,512]{0,1:T(8,128)S(1)}, u32[]{:S(2)}, u32[]{:S(2)}) %collective-permute-start.7) | collective-permute-done | bytes 524320 | tf_op jit(solution)/shard_map/ppermute | solution.py:14
  265.2 11.2 %collective-permute-done.8 = f32[256,512]{0,1:T(8,128)S(1)} collective-permute-done((f32[256,512]{0,1:T(8,128)}, f32[256,512]{0,1:T(8,128)S(1)}, u32[]{:S(2)}, u32[]{:S(2)}) %collective-permute-start.8) | collective-permute-done | bytes 524320 | tf_op jit(solution)/shard_map/ppermute | solution.py:14
  276.4 1.5 fusion.16
  277.9 2.4 pad_maximum_fusion
  280.3 5.5 %copy.70 = f32[2,1024,512]{2,1,0:T(8,128)} copy(f32[2,1024,512]{1,2,0:T(8,128)} %pad_maximum_fusion) | data formatting | bytes 8388608
  285.8 1.8 collective-permute-done.34
  287.7 8.7 %collective-permute-done.35 = f32[256,512]{0,1:T(8,128)} collective-permute-done((f32[256,512]{0,1:T(8,128)}, f32[256,512]{0,1:T(8,128)}, u32[]{:S(2)}, u32[]{:S(2)}) %collective-permute-start.35) | collective-permute-done | bytes 524320 | tf_op jit(solution)/shard_map/ppermute | solution.py:14
  296.3 2.1 bitcast_dynamic-update-slice_fusion
  298.4 1.8 copy.71
  (130 shorter events, 42.3 us)
Async XLA Ops:
  0.6 157.7 %copy-start = (f32[1,1024,256]{2,1,0:T(8,128)S(1)}, f32[1,1024,256]{2,1,0:T(8,128)}, u32[]{:S(2)}) copy-start(f32[1,1024,256]{2,1,0:T(8,128)} %param.24) | copy-start | bytes 3145732
  2.6 42.9 %collective-permute-start.10 = (f32[256,256]{1,0:T(8,128)}, f32[256,256]{1,0:T(8,128)}, u32[]{:S(2)}, u32[]{:S(2)}) collective-permute-start(f32[256,256]{1,0:T(8,128)} %get-tuple-element.13), channel_id=1, source_target_pairs={{1,0},{3,2},{5,4},{7,6},{9,8},{11,10},{13,12},{15,14},{17,16},{19,... | collective-permute-start | bytes 786440 | tf_op jit(solution)/shard_map/ppermute | solution.py:14
  3.9 65.1 %collective-permute-start.12 = (f32[256,256]{1,0:T(8,128)}, f32[256,256]{1,0:T(8,128)}, u32[]{:S(2)}, u32[]{:S(2)}) collective-permute-start(f32[256,256]{1,0:T(8,128)} %get-tuple-element.13), channel_id=1, source_target_pairs={{2,0},{6,4},{10,8},{14,12},{18,16},{22,20},{26,24},{30,28}} | collective-permute-start | bytes 786440 | tf_op jit(solution)/shard_map/ppermute | solution.py:14
  5.2 105.9 %collective-permute-start.14 = (f32[256,256]{1,0:T(8,128)}, f32[256,256]{1,0:T(8,128)S(1)}, u32[]{:S(2)}, u32[]{:S(2)}) collective-permute-start(f32[256,256]{1,0:T(8,128)} %get-tuple-element.13), channel_id=1, source_target_pairs={{4,0},{12,8},{20,16},{28,24}} | collective-permute-start | bytes 786440 | tf_op jit(solution)/shard_map/ppermute | solution.py:14
  11.2 3.1 %copy-start.9 = (f32[2,1024,256]{2,1,0:T(8,128)S(1)}, f32[2,1024,256]{2,1,0:T(8,128)}, u32[]{:S(2)}) copy-start(f32[2,1024,256]{2,1,0:T(8,128)} %param.15) | copy-start | bytes 6291460
  14.2 3.4 %copy-start.24 = (s32[8]{0:T(128)S(1)}, s32[8]{0:T(128)}, u32[]{:S(2)}) copy-start(s32[8]{0:T(128)} %param.19) | copy-start | bytes 100
  21.6 3.3 %copy-start.6 = (f32[2,1,256,256]{3,2,1,0:T(8,128)S(1)}, f32[2,1,256,256]{3,2,1,0:T(8,128)}, u32[]{:S(2)}) copy-start(f32[2,1,256,256]{3,2,1,0:T(8,128)} %param.17) | copy-start | bytes 1572868
  21.6 7.1 %copy-start.5 = (f32[2,1024,512]{2,1,0:T(8,128)S(1)}, f32[2,1024,512]{2,1,0:T(8,128)}, u32[]{:S(2)}) copy-start(f32[2,1024,512]{2,1,0:T(8,128)} %param.14) | copy-start | bytes 12582916
  21.6 7.1 %copy-start.10 = (f32[2,1024,256]{2,1,0:T(8,128)S(1)}, f32[2,1024,256]{2,1,0:T(8,128)}, u32[]{:S(2)}) copy-start(f32[2,1024,256]{2,1,0:T(8,128)} %param.15) | copy-start | bytes 6291460
  26.1 20.8 %collective-permute-start.9 = (f32[256,512]{0,1:T(8,128)}, f32[256,512]{0,1:T(8,128)}, u32[]{:S(2)}, u32[]{:S(2)}) collective-permute-start(f32[256,512]{0,1:T(8,128)} %convolution_bitcast_fusion.7), channel_id=1, source_target_pairs={{1,0},{3,2},{5,4},{7,6},{9,8},{11,10},{13,12},{15,14},{17,16},{19,... | collective-permute-start | bytes 1572872 | tf_op jit(solution)/shard_map/ppermute | solution.py:14
  27.4 22.8 %collective-permute-start.1 = (f32[256,256]{1,0:T(8,128)}, f32[256,256]{1,0:T(8,128)}, u32[]{:S(2)}, u32[]{:S(2)}) collective-permute-start(f32[256,256]{1,0:T(8,128)} %get-tuple-element.12), channel_id=1, source_target_pairs={{1,0},{3,2},{5,4},{7,6},{9,8},{11,10},{13,12},{15,14},{17,16},{19,... | collective-permute-start | bytes 786440 | tf_op jit(solution)/shard_map/ppermute | solution.py:14
  30.6 6.0 %copy-start.25 = (s32[4]{0:T(128)S(1)}, s32[4]{0:T(128)}, u32[]{:S(2)}) copy-start(s32[4]{0:T(128)} %param.21) | copy-start | bytes 52
  30.6 6.0 %copy-start.26 = (s32[8,1]{0,1:T(1,128)S(1)}, s32[8,1]{0,1:T(1,128)}, u32[]{:S(2)}) copy-start(s32[8,1]{0,1:T(1,128)} %param.20) | copy-start | bytes 100
  36.7 4.5 %copy-start.23 = (s32[8,128]{1,0:T(8,128)S(1)}, s32[8,128]{1,0:T(8,128)}, u32[]{:S(2)}) copy-start(s32[8,128]{1,0:T(8,128)} %param.22) | copy-start | bytes 12292
  43.9 5.8 %copy-start.7 = (f32[2,1,256,256]{3,2,1,0:T(8,128)S(1)}, f32[2,1,256,256]{3,2,1,0:T(8,128)}, u32[]{:S(2)}) copy-start(f32[2,1,256,256]{3,2,1,0:T(8,128)} %param.17) | copy-start | bytes 1572868
  45.5 19.9 %copy-start.1 = (f32[1024,512]{0,1:T(8,128)S(1)}, f32[1024,512]{0,1:T(8,128)}, u32[]{:S(2)}) copy-start(f32[1024,512]{0,1:T(8,128)} %subtract_select_fusion.1) | copy-start | bytes 6291460
  45.5 40.0 %collective-permute-start.3 = (f32[256,256]{1,0:T(8,128)}, f32[256,256]{1,0:T(8,128)S(1)}, u32[]{:S(2)}, u32[]{:S(2)}) collective-permute-start(f32[256,256]{1,0:T(8,128)} %get-tuple-element.12), channel_id=1, source_target_pairs={{2,0},{6,4},{10,8},{14,12},{18,16},{22,20},{26,24},{30,28}} | collective-permute-start | bytes 786440 | tf_op jit(solution)/shard_map/ppermute | solution.py:14
  47.0 17.2 %collective-permute-start = (f32[256,512]{0,1:T(8,128)S(1)}, f32[256,512]{0,1:T(8,128)S(1)}, u32[]{:S(2)}, u32[]{:S(2)}) collective-permute-start(f32[256,512]{0,1:T(8,128)S(1)} %convolution_bitcast_fusion.11), channel_id=1, source_target_pairs={{1,0},{3,2},{5,4},{7,6},{9,8},{11,10},{13,12},{15,14},{17,16},{19,... | collective-permute-start | bytes 1572872 | tf_op jit(solution)/shard_map/ppermute | solution.py:14
  49.8 31.1 %copy-start.19 = (f32[256,512]{0,1:T(8,128)}, f32[256,512]{0,1:T(8,128)S(1)}, u32[]{:S(2)}) copy-start(f32[256,512]{0,1:T(8,128)S(1)} %fusion.9) | copy-start | bytes 1572868
  50.2 69.7 %collective-permute-start.5 = (f32[256,256]{1,0:T(8,128)}, f32[256,256]{1,0:T(8,128)}, u32[]{:S(2)}, u32[]{:S(2)}) collective-permute-start(f32[256,256]{1,0:T(8,128)} %get-tuple-element.12), channel_id=1, source_target_pairs={{4,0},{12,8},{20,16},{28,24}} | collective-permute-start | bytes 786440 | tf_op jit(solution)/shard_map/ppermute | solution.py:14
  64.1 16.7 %collective-permute-start.11 = (f32[256,512]{0,1:T(8,128)S(1)}, f32[256,512]{0,1:T(8,128)S(1)}, u32[]{:S(2)}, u32[]{:S(2)}) collective-permute-start(f32[256,512]{0,1:T(8,128)S(1)} %convolution_bitcast_fusion.6), channel_id=1, source_target_pairs={{2,0},{6,4},{10,8},{14,12},{18,16},{22,20},{26,24},{30,28}} | collective-permute-start | bytes 1572872 | tf_op jit(solution)/shard_map/ppermute | solution.py:14
  69.0 32.6 %collective-permute-start.2 = (f32[256,512]{0,1:T(8,128)S(1)}, f32[256,512]{0,1:T(8,128)S(1)}, u32[]{:S(2)}, u32[]{:S(2)}) collective-permute-start(f32[256,512]{0,1:T(8,128)S(1)} %convolution_bitcast_fusion.10), channel_id=1, source_target_pairs={{2,0},{6,4},{10,8},{14,12},{18,16},{22,20},{26,24},{30,28}} | collective-permute-start | bytes 1572872 | tf_op jit(solution)/shard_map/ppermute | solution.py:14
  83.0 2.5 copy-start.18
  84.2 26.9 %collective-permute-start.13 = (f32[256,512]{0,1:T(8,128)}, f32[256,512]{0,1:T(8,128)}, u32[]{:S(2)}, u32[]{:S(2)}) collective-permute-start(f32[256,512]{0,1:T(8,128)} %convolution_bitcast_fusion.5), channel_id=1, source_target_pairs={{4,0},{12,8},{20,16},{28,24}} | collective-permute-start | bytes 1572872 | tf_op jit(solution)/shard_map/ppermute | solution.py:14
  104.0 1.2 copy-start.16
  105.2 15.3 %collective-permute-start.4 = (f32[256,512]{0,1:T(8,128)}, f32[256,512]{0,1:T(8,128)}, u32[]{:S(2)}, u32[]{:S(2)}) collective-permute-start(f32[256,512]{0,1:T(8,128)} %convolution_bitcast_fusion.9), channel_id=1, source_target_pairs={{4,0},{12,8},{20,16},{28,24}} | collective-permute-start | bytes 1572872 | tf_op jit(solution)/shard_map/ppermute | solution.py:14
  111.0 9.5 %copy-start.17 = (f32[256,512]{0,1:T(8,128)S(1)}, f32[256,512]{0,1:T(8,128)}, u32[]{:S(2)}) copy-start(f32[256,512]{0,1:T(8,128)} %copy-done.16) | copy-start | bytes 1572868
  113.7 11.8 %copy-start.12 = (f32[256,512]{0,1:T(8,128)}, f32[256,512]{0,1:T(8,128)S(1)}, u32[]{:S(2)}) copy-start(f32[256,512]{0,1:T(8,128)S(1)} %get-tuple-element.18) | copy-start | bytes 1572868
  113.8 11.6 %collective-permute-start.21 = (f32[64,512]{0,1:T(8,128)S(1)}, f32[64,512]{0,1:T(8,128)S(1)}, u32[]{:S(2)}, u32[]{:S(2)}) collective-permute-start(f32[64,512]{0,1:T(8,128)S(1)} %slice.128), channel_id=1, source_target_pairs={{0,4},{8,12},{16,20},{24,28}} | collective-permute-start | bytes 393224 | tf_op jit(solution)/shard_map/ppermute | solution.py:14
  122.8 14.1 %copy-start.14 = (f32[256,512]{0,1:T(8,128)}, f32[256,512]{0,1:T(8,128)S(1)}, u32[]{:S(2)}) copy-start(f32[256,512]{0,1:T(8,128)S(1)} %get-tuple-element.22) | copy-start | bytes 1572868
  122.9 8.2 %collective-permute-start.18 = (f32[64,512]{0,1:T(8,128)S(1)}, f32[64,512]{0,1:T(8,128)S(1)}, u32[]{:S(2)}, u32[]{:S(2)}) collective-permute-start(f32[64,512]{0,1:T(8,128)S(1)} %slice.122), channel_id=1, source_target_pairs={{0,4},{8,12},{16,20},{24,28}} | collective-permute-start | bytes 393224 | tf_op jit(solution)/shard_map/ppermute | solution.py:14
  125.6 11.2 %collective-permute-start.22 = (f32[32,512]{0,1:T(8,128)S(1)}, f32[32,512]{0,1:T(8,128)S(1)}, u32[]{:S(2)}, u32[]{:S(2)}) collective-permute-start(f32[32,512]{0,1:T(8,128)S(1)} %slice.130), channel_id=1, source_target_pairs={{0,2},{4,6},{8,10},{12,14},{16,18},{20,22},{24,26},{28,30}} | collective-permute-start | bytes 196616 | tf_op jit(solution)/shard_map/ppermute | solution.py:14
  131.3 9.3 %collective-permute-start.19 = (f32[32,512]{0,1:T(8,128)S(1)}, f32[32,512]{0,1:T(8,128)S(1)}, u32[]{:S(2)}, u32[]{:S(2)}) collective-permute-start(f32[32,512]{0,1:T(8,128)S(1)} %slice.124), channel_id=1, source_target_pairs={{0,2},{4,6},{8,10},{12,14},{16,18},{20,22},{24,26},{28,30}} | collective-permute-start | bytes 196616 | tf_op jit(solution)/shard_map/ppermute | solution.py:14
  136.9 6.6 %collective-permute-start.23 = (f32[16,512]{0,1:T(8,128)S(1)}, f32[16,512]{0,1:T(8,128)S(1)}, u32[]{:S(2)}, u32[]{:S(2)}) collective-permute-start(f32[16,512]{0,1:T(8,128)S(1)} %slice.132), channel_id=1, source_target_pairs={{0,1},{2,3},{4,5},{6,7},{8,9},{10,11},{12,13},{14,15},{16,17},{18,... | collective-permute-start | bytes 98312 | tf_op jit(solution)/shard_map/ppermute | solution.py:14
  141.5 6.3 %collective-permute-start.20 = (f32[16,512]{0,1:T(8,128)}, f32[16,512]{0,1:T(8,128)}, u32[]{:S(2)}, u32[]{:S(2)}) collective-permute-start(f32[16,512]{0,1:T(8,128)} %slice.126), channel_id=1, source_target_pairs={{0,1},{2,3},{4,5},{6,7},{8,9},{10,11},{12,13},{14,15},{16,17},{18,... | collective-permute-start | bytes 98312 | tf_op jit(solution)/shard_map/ppermute | solution.py:14
  149.6 4.1 %collective-permute-start.24 = (f32[2,16,512]{2,1,0:T(8,128)S(1)}, f32[2,16,512]{2,1,0:T(8,128)S(1)}, u32[]{:S(2)}, u32[]{:S(2)}) collective-permute-start(f32[2,16,512]{2,1,0:T(8,128)S(1)} %pad_maximum_fusion.1), channel_id=1, source_target_pairs={{0,8},{8,16},{16,24},{24,0},{1,9},{9,17},{17,25},{25,1},{2,10},{10... | collective-permute-start | bytes 196616 | tf_op jit(solution)/shard_map/ppermute | solution.py:14
  149.7 5.1 %collective-permute-start.25 = (f32[2,16,512]{2,1,0:T(8,128)S(1)}, f32[2,16,512]{2,1,0:T(8,128)S(1)}, u32[]{:S(2)}, u32[]{:S(2)}) collective-permute-start(f32[2,16,512]{2,1,0:T(8,128)S(1)} %pad_maximum_fusion.1), channel_id=1, source_target_pairs={{0,16},{8,24},{16,0},{24,8},{1,17},{9,25},{17,1},{25,9},{2,18},{10... | collective-permute-start | bytes 196616 | tf_op jit(solution)/shard_map/ppermute | solution.py:14
  152.3 3.3 %collective-permute-start.26 = (f32[2,16,512]{2,1,0:T(8,128)S(1)}, f32[2,16,512]{2,1,0:T(8,128)S(1)}, u32[]{:S(2)}, u32[]{:S(2)}) collective-permute-start(f32[2,16,512]{2,1,0:T(8,128)S(1)} %pad_maximum_fusion.1), channel_id=1, source_target_pairs={{0,24},{8,0},{16,8},{24,16},{1,25},{9,1},{17,9},{25,17},{2,26},{10... | collective-permute-start | bytes 196616 | tf_op jit(solution)/shard_map/ppermute | solution.py:14
  158.3 1.0 copy-start.22
  159.8 2.4 copy-start.21
  160.8 1.3 copy-start.3
  163.3 23.3 %collective-permute-start.27 = (f32[256,512]{0,1:T(8,128)}, f32[256,512]{0,1:T(8,128)}, u32[]{:S(2)}, u32[]{:S(2)}) collective-permute-start(f32[256,512]{0,1:T(8,128)} %convolution_bitcast_fusion.3), channel_id=1, source_target_pairs={{1,0},{3,2},{5,4},{7,6},{9,8},{11,10},{13,12},{15,14},{17,16},{19,... | collective-permute-start | bytes 1572872 | tf_op jit(solution)/shard_map/ppermute | solution.py:14
  164.6 22.0 %collective-permute-start.28 = (f32[256,256]{1,0:T(8,128)}, f32[256,256]{1,0:T(8,128)}, u32[]{:S(2)}, u32[]{:S(2)}) collective-permute-start(f32[256,256]{1,0:T(8,128)} %bitcast.47), channel_id=1, source_target_pairs={{1,0},{3,2},{5,4},{7,6},{9,8},{11,10},{13,12},{15,14},{17,16},{19,... | collective-permute-start | bytes 786440 | tf_op jit(solution)/shard_map/ppermute | solution.py:14
  188.3 0.8 copy-start.20
  191.3 21.8 %collective-permute-start.29 = (f32[256,512]{0,1:T(8,128)}, f32[256,512]{0,1:T(8,128)}, u32[]{:S(2)}, u32[]{:S(2)}) collective-permute-start(f32[256,512]{0,1:T(8,128)} %convolution_bitcast_fusion.2), channel_id=1, source_target_pairs={{2,0},{6,4},{10,8},{14,12},{18,16},{22,20},{26,24},{30,28}} | collective-permute-start | bytes 1572872 | tf_op jit(solution)/shard_map/ppermute | solution.py:14
  192.6 20.5 %collective-permute-start.30 = (f32[256,256]{1,0:T(8,128)}, f32[256,256]{1,0:T(8,128)}, u32[]{:S(2)}, u32[]{:S(2)}) collective-permute-start(f32[256,256]{1,0:T(8,128)} %bitcast.47), channel_id=1, source_target_pairs={{2,0},{6,4},{10,8},{14,12},{18,16},{22,20},{26,24},{30,28}} | collective-permute-start | bytes 786440 | tf_op jit(solution)/shard_map/ppermute | solution.py:14
  193.9 48.1 %collective-permute-start.15 = (f32[256,512]{0,1:T(8,128)}, f32[256,512]{0,1:T(8,128)}, u32[]{:S(2)}, u32[]{:S(2)}) collective-permute-start(f32[256,512]{0,1:T(8,128)} %copy-done.19), channel_id=1, source_target_pairs={{0,1},{2,3},{4,5},{6,7},{8,9},{10,11},{12,13},{14,15},{16,17},{18,... | collective-permute-start | bytes 1572872 | tf_op jit(solution)/shard_map/ppermute | solution.py:14
  216.0 0.8 copy-start.11
  218.0 25.5 %collective-permute-start.31 = (f32[256,512]{0,1:T(8,128)}, f32[256,512]{0,1:T(8,128)}, u32[]{:S(2)}, u32[]{:S(2)}) collective-permute-start(f32[256,512]{0,1:T(8,128)} %convolution_bitcast_fusion.1), channel_id=1, source_target_pairs={{4,0},{12,8},{20,16},{28,24}} | collective-permute-start | bytes 1572872 | tf_op jit(solution)/shard_map/ppermute | solution.py:14
  219.3 20.5 %collective-permute-start.32 = (f32[256,256]{1,0:T(8,128)}, f32[256,256]{1,0:T(8,128)}, u32[]{:S(2)}, u32[]{:S(2)}) collective-permute-start(f32[256,256]{1,0:T(8,128)} %bitcast.47), channel_id=1, source_target_pairs={{4,0},{12,8},{20,16},{28,24}} | collective-permute-start | bytes 786440 | tf_op jit(solution)/shard_map/ppermute | solution.py:14
  220.6 27.0 %collective-permute-start.6 = (f32[256,512]{0,1:T(8,128)}, f32[256,512]{0,1:T(8,128)}, u32[]{:S(2)}, u32[]{:S(2)}) collective-permute-start(f32[256,512]{0,1:T(8,128)} %fusion.12), channel_id=1, source_target_pairs={{0,1},{2,3},{4,5},{6,7},{8,9},{10,11},{12,13},{14,15},{16,17},{18,... | collective-permute-start | bytes 1572872 | tf_op jit(solution)/shard_map/ppermute | solution.py:14
  222.7 27.0 %collective-permute-start.16 = (f32[256,512]{0,1:T(8,128)}, f32[256,512]{0,1:T(8,128)}, u32[]{:S(2)}, u32[]{:S(2)}) collective-permute-start(f32[256,512]{0,1:T(8,128)} %get-tuple-element.17), channel_id=1, source_target_pairs={{0,2},{4,6},{8,10},{12,14},{16,18},{20,22},{24,26},{28,30}} | collective-permute-start | bytes 1572872 | tf_op jit(solution)/shard_map/ppermute | solution.py:14
  239.8 14.1 %collective-permute-start.17 = (f32[256,512]{0,1:T(8,128)}, f32[256,512]{0,1:T(8,128)}, u32[]{:S(2)}, u32[]{:S(2)}) collective-permute-start(f32[256,512]{0,1:T(8,128)} %get-tuple-element.19), channel_id=1, source_target_pairs={{0,4},{8,12},{16,20},{24,28}} | collective-permute-start | bytes 1572872 | tf_op jit(solution)/shard_map/ppermute | solution.py:14
  242.1 18.0 %copy-start.13 = (f32[256,512]{0,1:T(8,128)S(1)}, f32[256,512]{0,1:T(8,128)}, u32[]{:S(2)}) copy-start(f32[256,512]{0,1:T(8,128)} %copy-done.12) | copy-start | bytes 1572868
  242.1 23.1 %collective-permute-start.7 = (f32[256,512]{0,1:T(8,128)}, f32[256,512]{0,1:T(8,128)S(1)}, u32[]{:S(2)}, u32[]{:S(2)}) collective-permute-start(f32[256,512]{0,1:T(8,128)} %get-tuple-element.21), channel_id=1, source_target_pairs={{0,2},{4,6},{8,10},{12,14},{16,18},{20,22},{24,26},{28,30}} | collective-permute-start | bytes 1572872 | tf_op jit(solution)/shard_map/ppermute | solution.py:14
  243.5 32.9 %copy-start.2 = (f32[1024,512]{0,1:T(8,128)S(1)}, f32[1024,512]{0,1:T(8,128)}, u32[]{:S(2)}) copy-start(f32[1024,512]{0,1:T(8,128)} %subtract_select_fusion.1) | copy-start | bytes 6291460
  243.6 32.9 %copy-start.8 = (f32[2,1,256,256]{3,2,1,0:T(8,128)S(1)}, f32[2,1,256,256]{3,2,1,0:T(8,128)}, u32[]{:S(2)}) copy-start(f32[2,1,256,256]{3,2,1,0:T(8,128)} %param.17) | copy-start | bytes 1572868
  243.6 32.9 %copy-start.15 = (f32[256,512]{0,1:T(8,128)S(1)}, f32[256,512]{0,1:T(8,128)}, u32[]{:S(2)}) copy-start(f32[256,512]{0,1:T(8,128)} %copy-done.14) | copy-start | bytes 1572868
  243.6 32.8 %collective-permute-start.8 = (f32[256,512]{0,1:T(8,128)}, f32[256,512]{0,1:T(8,128)S(1)}, u32[]{:S(2)}, u32[]{:S(2)}) collective-permute-start(f32[256,512]{0,1:T(8,128)} %get-tuple-element.23), channel_id=1, source_target_pairs={{0,4},{8,12},{16,20},{24,28}} | collective-permute-start | bytes 1572872 | tf_op jit(solution)/shard_map/ppermute | solution.py:14
  247.6 38.2 %collective-permute-start.33 = (f32[256,512]{0,1:T(8,128)}, f32[256,512]{0,1:T(8,128)}, u32[]{:S(2)}, u32[]{:S(2)}) collective-permute-start(f32[256,512]{0,1:T(8,128)} %copy-done.20), channel_id=1, source_target_pairs={{0,1},{2,3},{4,5},{6,7},{8,9},{10,11},{12,13},{14,15},{16,17},{18,... | collective-permute-start | bytes 1572872 | tf_op jit(solution)/shard_map/ppermute | solution.py:14
  249.7 37.9 %collective-permute-start.34 = (f32[256,512]{0,1:T(8,128)}, f32[256,512]{0,1:T(8,128)}, u32[]{:S(2)}, u32[]{:S(2)}) collective-permute-start(f32[256,512]{0,1:T(8,128)} %get-tuple-element.25), channel_id=1, source_target_pairs={{0,2},{4,6},{8,10},{12,14},{16,18},{20,22},{24,26},{28,30}} | collective-permute-start | bytes 1572872 | tf_op jit(solution)/shard_map/ppermute | solution.py:14
  254.0 42.4 %collective-permute-start.35 = (f32[256,512]{0,1:T(8,128)}, f32[256,512]{0,1:T(8,128)}, u32[]{:S(2)}, u32[]{:S(2)}) collective-permute-start(f32[256,512]{0,1:T(8,128)} %fusion.4), channel_id=1, source_target_pairs={{0,4},{8,12},{16,20},{24,28}} | collective-permute-start | bytes 1572872 | tf_op jit(solution)/shard_map/ppermute | solution.py:14
  280.3 16.0 %copy-start.4 = (f32[1024,512]{0,1:T(8,128)S(1)}, f32[1024,512]{0,1:T(8,128)}, u32[]{:S(2)}) copy-start(f32[1024,512]{0,1:T(8,128)} %copy-done.3) | copy-start | bytes 6291460

commit v2 on v0

v2 whole, which is shorter than its diff:
```python
import functools

import jax
import jax.numpy as jnp
from jax import lax
from jax.experimental import pallas as pl
from jax.experimental.pallas import tpu as pltpu
from jax.sharding import PartitionSpec as P

NPIV = 128
CHUNK = 256
F32 = jnp.float32
BF16 = jnp.bfloat16


def split(x):
    high = x.astype(BF16)
    return high, (x - high.astype(F32)).astype(BF16)


def dot3(a, b, side):
    (ah, al), (bh, bl) = a, b
    dims = (((side,), (0,)), ((), ()))
    one = functools.partial(lax.dot_general, dimension_numbers=dims, preferred_element_type=F32)
    return one(ah, bh) + (one(ah, bl) + one(al, bh))


class Front:
    def __init__(self, blocks, x, vec, fac, nvec, nfac_any, s):
        self.blocks, self.levels = blocks, blocks.bit_length() - 1
        self.x, self.vec, self.fac, self.nvec, self.nfac_any = x, vec, fac, nvec, nfac_any
        (self.top, self.body, self.usend, self.urecv, self.wsend, self.wrecv, self.fin, self.lead,
         self.us, self.ur, self.ws, self.wr, self.gs, self.gr, self.fs) = s
        self.halves = x.shape[2] // CHUNK
        self.chunks = x.shape[0] * self.halves
        self.width = fac.shape[-1]
        self.place = lax.axis_index("rows")

    def role(self, level):
        step = 1 << level
        return self.place % (2 * step) == 0, self.place % (2 * step) == step, step

    def factor_copy(self, level, f, peer):
        return pltpu.make_async_remote_copy(
            self.nfac_any.at[f, 0], self.lead.at[level, f], self.gs.at[f], self.gr.at[level, f],
            device_id={"rows": peer}, device_id_type=pl.DeviceIdType.MESH)

    def send_factors(self):
        for level in range(self.levels):
            _, follow, step = self.role(level)

            @pl.when(follow)
            def _():
                for f in range(self.x.shape[0]):
                    self.factor_copy(level, f, self.place - step).start()

    def wait_factors(self):
        for level in range(self.levels):
            lead, _, step = self.role(level)

            @pl.when(lead)
            def _():
                for f in range(self.x.shape[0]):
                    self.factor_copy(level, f, self.place).wait_recv()

    def up_copy(self, level, c, peer):
        return pltpu.make_async_remote_copy(
            self.usend.at[c], self.urecv.at[level, c], self.us.at[c], self.ur.at[level, c],
            device_id={"rows": peer}, device_id_type=pl.DeviceIdType.MESH)

    def back_copy(self, level, c, peer):
        return pltpu.make_async_remote_copy(
            self.wsend.at[level, c], self.wrecv.at[c], self.ws.at[level, c], self.wr.at[c],
            device_id={"rows": peer}, device_id_type=pl.DeviceIdType.MESH)

    def send_up(self, level, c):
        _, follow, step = self.role(level)

        @pl.when(follow)
        def _():
            f = c // self.halves
            self.usend[c] = dot3(split(self.nvec[f, 0]), split(self.top[c]), 0)
            self.up_copy(level, c, self.place - step).start()

    def block(self, c, live):
        f, h = c // self.halves, c % self.halves
        columns = pl.ds(pl.multiple_of(h * CHUNK, CHUNK), CHUNK)
        x = self.x[f, :, columns]
        y = split(self.vec[f])
        project = dot3(y, split(x), 0)
        scaled = dot3(split(self.fac[f, 0]), split(project), 0)
        if live is not None:
            scaled = jnp.where(self.place < live(f), scaled, 0.0)
        z = split(scaled)
        w = self.width
        self.top[c] = x[:w] - dot3((y[0][:w], y[1][:w]), z, 1)
        self.body[c] = x[w:] - dot3((y[0][w:], y[1][w:]), z, 1)
        self.send_up(0, c)

    def climb(self, c, live):
        f = c // self.halves
        for level in range(self.levels):
            lead, _, step = self.role(level)
            if level:
                self.send_up(level, c)

            @pl.when(lead)
            def _():
                peer = self.place + step
                self.up_copy(level, c, peer).wait_recv()
                top = self.top[c]
                weight = dot3(split(self.lead[level, f]), split(top + self.urecv[level, c]), 0)
                if live is not None:
                    weight = jnp.where(peer < live(f), weight, 0.0)
                self.wsend[level, c] = weight
                self.back_copy(level, c, peer).start()
                self.top[c] = top - weight

    def finish(self, c, cut):
        f = c // self.halves

        @pl.when(self.place == 0)
        def _():
            top = self.top[c]
            if cut:
                rows = lax.broadcasted_iota(jnp.int32, top.shape, 0)
                top = jnp.where(rows < NPIV, top, 0.0)
            self.fin[c] = top

        @pl.when(self.place != 0)
        def _():
            self.back_copy(0, c, self.place).wait_recv()
            weight = split(self.wrecv[c])
            self.fin[c] = self.top[c] - dot3(split(self.nvec[f, 0]), weight, 1)

    def result_copies(self, out, c):
        f, h = c // self.halves, c % self.halves
        columns = pl.ds(pl.multiple_of(h * CHUNK, CHUNK), CHUNK)
        w, rows = self.width, self.x.shape[1]
        return (
            pltpu.make_async_copy(self.body.at[c], out.at[f, pl.ds(w, rows - w), columns], self.fs.at[0, c]),
            pltpu.make_async_copy(self.fin.at[c], out.at[f, pl.ds(0, w), columns], self.fs.at[1, c]),
        )

    def drain(self, out):
        for level in range(self.levels):
            lead, follow, _ = self.role(level)

            @pl.when(lead)
            def _():
                @pl.loop(0, self.chunks)
                def _(c):
                    self.back_copy(level, c, self.place).wait_send()

            @pl.when(follow)
            def _():
                for f in range(self.x.shape[0]):
                    self.factor_copy(level, f, self.place).wait_send()

                @pl.loop(0, self.chunks)
                def _(c):
                    self.up_copy(level, c, self.place).wait_send()

        @pl.loop(0, self.chunks)
        def _(c):
            for copy in self.result_copies(out, c):
                copy.wait()


def front_scratch(fronts, rows, cols, width, levels):
    chunks = fronts * (cols // CHUNK)
    piece = (width, CHUNK)
    dma = pltpu.SemaphoreType.DMA
    return [
        pltpu.VMEM((chunks,) + piece, F32),
        pltpu.VMEM((chunks, rows - width, CHUNK), F32),
        pltpu.VMEM((chunks,) + piece, F32),
        pltpu.VMEM((levels, chunks) + piece, F32),
        pltpu.VMEM((levels, chunks) + piece, F32),
        pltpu.VMEM((chunks,) + piece, F32),
        pltpu.VMEM((chunks,) + piece, F32),
        pltpu.VMEM((levels, fronts, width, width), F32),
        dma((chunks,)), dma((levels, chunks)), dma((levels, chunks)), dma((chunks,)),
        dma((fronts,)), dma((levels, fronts)), dma((2, chunks)),
    ]


def kernel(blocks, columns, rows_ref, live_ref, lx, lv, lf, mv, mf, ux, uv, uf, sv, sf, out_low, out_up, *s):
    place, column = lax.axis_index("rows"), lax.axis_index("fronts")
    vlx, vlv, vlf, vmv, vux, vuv, vuf, vsv, portions, load_sem, part_s, part_r, over_s, over_r = s[:14]
    low = Front(blocks, vlx, vlv, vlf, vmv, mf, s[14:29])
    up = Front(blocks, vux, vuv, vuf, vsv, sf, s[29:44])
    fronts = lx.shape[0]
    share = portions.shape[3]

    pairs = []
    for f in range(fronts):
        pairs += [(lx.at[f], vlx.at[f]), (lv.at[f], vlv.at[f]), (lf.at[f], vlf.at[f]), (mv.at[f], vmv.at[f])]
    first = len(pairs)
    pairs += [(ux, vux), (uv, vuv), (uf, vuf), (sv, vsv)]
    loads = [pltpu.make_async_copy(a, b, load_sem.at[i]) for i, (a, b) in enumerate(pairs)]
    for copy in loads:
        copy.start()

    barrier = pltpu.get_barrier_semaphore()
    for shift in range(1, blocks):
        pl.semaphore_signal(barrier, inc=1, device_id={"rows": (place + shift) % blocks},
                            device_id_type=pl.DeviceIdType.MESH)
    for shift in range(1, columns):
        pl.semaphore_signal(barrier, inc=1, device_id={"fronts": (column + shift) % columns},
                            device_id_type=pl.DeviceIdType.MESH)
    pl.semaphore_wait(barrier, blocks + columns - 2)
    low.send_factors()
    up.send_factors()

    def live(f):
        return live_ref[column * fronts + f]

    for copy in loads[:first]:
        copy.wait()

    @pl.loop(0, low.chunks)
    def _(c):
        low.block(c, live)
        low.result_copies(out_low, c)[0].start()

    low.wait_factors()

    def part(c, r, peer):
        f, h = c // low.halves, c % low.halves
        return pltpu.make_async_remote_copy(
            low.top.at[c, pl.ds(NPIV + r * share, share)], portions.at[column, f, h],
            part_s.at[r, c], part_r.at[c], device_id={"rows": peer}, device_id_type=pl.DeviceIdType.MESH)

    def over(c, shift, peer, slot):
        f, h = c // low.halves, c % low.halves
        return pltpu.make_async_remote_copy(
            portions.at[slot, f, h], portions.at[slot, f, h], over_s.at[shift, c], over_r.at[shift, c],
            device_id={"fronts": peer}, device_id_type=pl.DeviceIdType.MESH)

    @pl.loop(0, low.chunks)
    def _(c):
        low.climb(c, live)

        @pl.when(place == 0)
        def _():
            for r in range(1, blocks):
                part(c, r, r).start()
            portions[column, c // low.halves, c % low.halves] = low.top[c, pl.ds(NPIV, share)]

    for copy in loads[first:]:
        copy.wait()

    @pl.loop(0, low.chunks)
    def _(c):
        @pl.when(place != 0)
        def _():
            part(c, 0, place).wait_recv()

        for shift in range(1, columns):
            over(c, shift, (column + shift) % columns, column).start()

    @pl.loop(0, low.chunks)
    def _(c):
        low.finish(c, True)
        low.result_copies(out_low, c)[1].start()

    up.wait_factors()

    @pl.loop(0, low.chunks)
    def _(c):
        for shift in range(1, columns):
            over(c, shift, column, (column - shift + columns) % columns).wait_recv()

    height = vux.shape[1]
    here = rows_ref[...]
    hit = lax.broadcasted_iota(jnp.int32, (height, here.shape[1]), 0) == here
    chosen = jnp.where(hit, 1.0, 0.0)
    taken = jnp.sum(chosen, axis=1, keepdims=True) > 0.0
    chosen = chosen.astype(BF16)
    for h in range(low.halves):
        arrived = split(portions[:, :, h].reshape(here.shape[1], CHUNK))
        moved = jnp.dot(chosen, arrived[0], preferred_element_type=F32) + jnp.dot(
            chosen, arrived[1], preferred_element_type=F32)
        span = slice(h * CHUNK, (h + 1) * CHUNK)
        vux[0, :, span] = jnp.where(taken, moved, vux[0, :, span])

    @pl.loop(0, up.chunks)
    def _(c):
        up.block(c, None)
        up.result_copies(out_up, c)[0].start()

    @pl.loop(0, up.chunks)
    def _(c):
        up.climb(c, None)

    @pl.loop(0, up.chunks)
    def _(c):
        up.finish(c, False)
        up.result_copies(out_up, c)[1].start()

    @pl.when(place == 0)
    def _():
        @pl.loop(0, low.chunks)
        def _(c):
            for r in range(1, blocks):
                part(c, r, r).wait_send()

    @pl.loop(0, low.chunks)
    def _(c):
        for shift in range(1, columns):
            over(c, shift, column, column).wait_send()

    low.drain(out_low)
    up.drain(out_up)


def per_device(
    lower_rhs,
    lower_vectors,
    lower_factors,
    merge_vectors,
    merge_factors,
    live_blocks,
    parent_front,
    front_owner,
    contrib_rows,
    upper_rhs,
    upper_vectors,
    upper_factors,
    summit_vectors,
    summit_factors,
):
    place = lax.axis_index("rows")
    column = lax.axis_index("fronts")
    blocks = lax.axis_size("rows")
    columns = lax.axis_size("fronts")
    fronts, height, cols = lower_rhs.shape
    width = lower_factors.shape[-1]
    share = (width - NPIV) // blocks
    levels = blocks.bit_length() - 1
    parents = jnp.arange(front_owner.shape[0], dtype=jnp.int32)
    target = jnp.sum(jnp.where(parent_front == parents[None, :], front_owner[None, :], 0), axis=1)
    rows_here = lax.dynamic_slice_in_dim(contrib_rows, place * share, share, 1) - place * height
    rows_here = jnp.where((target == column)[:, None], rows_here, -1).reshape(1, -1)
    dma = pltpu.SemaphoreType.DMA
    chunks = fronts * (cols // CHUNK)
    held = [lower_rhs, lower_vectors, lower_factors, merge_vectors, upper_rhs, upper_vectors, upper_factors, summit_vectors]
    scratch = [pltpu.VMEM(a.shape, F32) for a in held]
    scratch += [
        pltpu.VMEM((columns, fronts, cols // CHUNK, share, CHUNK), F32),
        dma((4 * fronts + 4,)),
        dma((blocks, chunks)), dma((chunks,)), dma((columns, chunks)), dma((columns, chunks)),
    ]
    scratch += front_scratch(fronts, height, cols, width, levels)
    scratch += front_scratch(upper_rhs.shape[0], height, cols, width, levels)
    anywhere = pl.BlockSpec(memory_space=pl.ANY)
    return pl.pallas_call(
        functools.partial(kernel, blocks, columns),
        out_shape=(
            jax.ShapeDtypeStruct(lower_rhs.shape, F32),
            jax.ShapeDtypeStruct(upper_rhs.shape, F32),
        ),
        in_specs=[pl.BlockSpec(memory_space=pltpu.VMEM), pl.BlockSpec(memory_space=pltpu.SMEM)] + [anywhere] * 10,
        out_specs=(anywhere, anywhere),
        scratch_shapes=scratch,
        compiler_params=pltpu.CompilerParams(
            collective_id=0, has_side_effects=True, vmem_limit_bytes=56 * 1024 * 1024),
        name="two_level",
    )(rows_here, live_blocks, lower_rhs, lower_vectors, lower_factors, merge_vectors, merge_factors,
      upper_rhs, upper_vectors, upper_factors, summit_vectors, summit_factors)


def solution(mesh):
    placed = (
        P("fronts", "rows", None),
        P("fronts", "rows", None),
        P("fronts", "rows", None, None),
        P("fronts", "rows", None, None),
        P("fronts", "rows", None, None),
        P(),
        P(),
        P(),
        P(),
        P("fronts", "rows", None),
        P("fronts", "rows", None),
        P("fronts", "rows", None, None),
        P("fronts", "rows", None, None),
        P("fronts", "rows", None, None),
    )
    return jax.shard_map(
        per_device,
        mesh=mesh,
        in_specs=placed,
        out_specs=(P("fronts", "rows", None), P("fronts", "rows", None)),
        check_vma=False,
    )
```

time: 424 us -> 185 us (0.44)
  waiting for transfers between devices: 287 us -> 0 us
  Pallas kernels: 0 us -> 176 us
  matrix products: 45.4 us -> 0 us
  starting transfers between devices: 31.5 us -> 0 us
  local copies, waits for them, and re-layouts: 29.7 us -> 6.71 us
  between operations: 14.6 us -> 0.65 us
  other arithmetic: 15.1 us -> 1.52 us
    ppermute x24 -> x0, waiting for transfers between devices: 197 us -> none  [partner(): return lax.ppermute(value, axis, pairs)]
    pallas_call x0 -> x1, Pallas kernels: none -> 176 us  [per_device(): pl.pallas_call(functools.partial(kernel, blocks, columns), out_shape=(jax...]
    psum x1 -> x0, waiting for transfers between devices: 71.6 us -> none  [from_root(): return lax.psum(kept, axis)]
    dot_general x25 -> x0, matrix products: 45.4 us -> none  [the longest x2 10.3 us: wy_apply(): project = jnp.einsum('fri,frn->fin', vectors, values, precision=EXACT)]
    ppermute x24 -> x0, starting transfers between devices: 31.4 us -> none  [partner(): return lax.ppermute(value, axis, pairs)]
    all_gather x1 -> x0, waiting for transfers between devices: 18.4 us -> none  [per_device(): gathered = lax.all_gather(shared, 'fronts', axis=0, tiled=True)]
    unnamed x52 -> x4, local copies, waits for them, and re-layouts: 21.5 us -> 6.11 us
    select_n x14 -> x1, other arithmetic: 8.42 us -> 0.76 us  [per_device(): jnp.where((target == column)[:, None], rows_here, -1).reshape(1, -1)]
  transfers between devices with their start and end apart: 26 -> 0, of which waited for: 20 -> 0; matrix products, arithmetic and copies ran while one was open for 9% -> 0% of each run, Pallas kernels for 0% -> 0%
where the time goes in v2:
time: 185 us
  Pallas kernels  176 us (95%)
  local copies, waits for them, and re-layouts  6.71 us (4%)
    pallas_call x1, Pallas kernels, per_device(): pl.pallas_call(functools.partial(kernel, blocks, columns), out_shape=(jax...  176 us
    unnamed x4, local copies, waits for them, and re-layouts  6.11 us

profile of v2, /device:TPU:0, one launch (start us, length us, event | category | flops | bytes accessed | tf_op | source)
XLA Modules:
  0.0 184.8 jit_solution(13646043795299869841)
XLA Ops:
  0.6 0.8 select_reduce_fusion
  1.4 0.8 subtract_select_fusion
  2.2 0.6 reshape.11.rows_ref
  2.8 176.0 %two_level.1 = (f32[2,1024,512]{2,1,0:T(8,128)}, f32[1,1024,512]{2,1,0:T(8,128)}) custom-call(s32[1,128]{1,0:T(1,128)} %reshape.11.rows_ref, s32[8]{0:T(128)} %live_ref.1, f32[2,1024,512]{2,1,0:T(8,128)} %lx.1, f32[2,1024,256]{2,1,0:T(8,128)} %lv.1, f32[2,1,256,256]{3,2,1,0:T(8,128)} %lf.1, f32[2,1,256,256]{3,2,1,0:T(8,128)} %mv.1, f32[2,1,256,256]{3,2,1,0:T(8,128)} %mf.1, ...), custom_call_target="tpu_custom_call" | custom-call | tf_op jit(solution)/shard_map/two_level/pallas_call | solution.py:358
  178.7 0.0 copy-start
  178.7 4.8 %copy.18 = f32[2,1024,512]{2,1,0:T(8,128)} copy(f32[2,1024,512]{2,1,0:T(8,128)} %get-tuple-element.4) | data formatting | bytes 8388608
  183.5 0.0 copy-done
  183.5 1.3 copy.19
  (1 shorter events, 0.0 us)
Async XLA Ops:
  178.7 4.8 %copy-start = (f32[1,1024,512]{2,1,0:T(8,128)S(1)}, f32[1,1024,512]{2,1,0:T(8,128)}, u32[]{:S(2)}) copy-start(f32[1,1024,512]{2,1,0:T(8,128)} %get-tuple-element.5) | copy-start | bytes 6291460

commit v3 on v2

v3 whole, which is shorter than its diff:
```python
import functools

import jax
import jax.numpy as jnp
from jax import lax
from jax.experimental import pallas as pl
from jax.experimental.pallas import tpu as pltpu
from jax.sharding import PartitionSpec as P

NPIV = 128
LOW_CHUNK = 256
UP_CHUNK = 128
F32 = jnp.float32
BF16 = jnp.bfloat16


def split(x):
    high = x.astype(BF16)
    return high, (x - high.astype(F32)).astype(BF16)


def dot3(a, b, side):
    (ah, al), (bh, bl) = a, b
    dims = (((side,), (0,)), ((), ()))
    one = functools.partial(lax.dot_general, dimension_numbers=dims, preferred_element_type=F32)
    return one(ah, bh) + (one(ah, bl) + one(al, bh))


class Front:
    def __init__(self, blocks, x, vec, fac, nvec, nfac, nfac_any, chunk, s):
        self.blocks, self.levels, self.chunk = blocks, blocks.bit_length() - 1, chunk
        self.x, self.vec, self.fac, self.nvec, self.nfac, self.nfac_any = x, vec, fac, nvec, nfac, nfac_any
        (self.top, self.body, self.usend, self.urecv, self.wsend, self.wrecv, self.fin, self.hold,
         self.lead_in, self.rest_in, self.first,
         self.us, self.ur, self.ws, self.wr, self.ts, self.hs, self.li, self.ri,
         self.gs, self.gr, self.fs) = s
        self.halves = x.shape[2] // chunk
        self.chunks = x.shape[0] * self.halves
        self.width = fac.shape[-1]
        self.place = lax.axis_index("rows")
        self.odd = self.place % 2 == 1

    def remote(self, src, dst, send, recv, peer):
        return pltpu.make_async_remote_copy(
            src, dst, send, recv, device_id={"rows": peer}, device_id_type=pl.DeviceIdType.MESH)

    def factor_copy(self, f, peer):
        return self.remote(self.nfac_any.at[f, 0], self.first.at[f], self.gs.at[f], self.gr.at[f], peer)

    def send_factors(self):
        @pl.when(self.odd)
        def _():
            for f in range(self.x.shape[0]):
                self.factor_copy(f, self.place - 1).start()

    def wait_factors(self):
        @pl.when(~self.odd)
        def _():
            for f in range(self.x.shape[0]):
                self.factor_copy(f, self.place).wait_recv()

    def up_copy(self, c, peer):
        return self.remote(self.usend.at[c], self.urecv.at[c], self.us.at[c], self.ur.at[c], peer)

    def back_copy(self, c, peer):
        return self.remote(self.wsend.at[c], self.wrecv.at[c], self.ws.at[c], self.wr.at[c], peer)

    def top_copy(self, c, peer):
        return self.remote(self.top.at[c], self.lead_in.at[c], self.ts.at[c], self.li.at[c], peer)

    def lead_copy(self, c, peer):
        return self.remote(self.hold.at[c], self.lead_in.at[c], self.hs.at[c], self.li.at[c], peer)

    def rest_copy(self, c, peer):
        return self.remote(self.hold.at[c], self.rest_in.at[c], self.hs.at[c], self.ri.at[c], peer)

    def home_copy(self, c, rows):
        span = pl.ds(0, rows)
        return self.remote(self.hold.at[c, span], self.rest_in.at[c, span], self.hs.at[c], self.ri.at[c], 0)

    def block(self, c, live):
        f, h = c // self.halves, c % self.halves
        columns = pl.ds(pl.multiple_of(h * self.chunk, self.chunk), self.chunk)
        x = self.x[f, :, columns]
        y = split(self.vec[f])
        project = dot3(y, split(x), 0)
        scaled = dot3(split(self.fac[f, 0]), split(project), 0)
        if live is not None:
            scaled = jnp.where(self.place < live(f), scaled, 0.0)
        z = split(scaled)
        w = self.width
        self.top[c] = x[:w] - dot3((y[0][:w], y[1][:w]), z, 1)

        @pl.when(self.odd)
        def _():
            self.usend[c] = dot3(split(self.nvec[f, 0]), split(self.top[c]), 0)
            self.up_copy(c, self.place - 1).start()

        self.body[c] = x[w:] - dot3((y[0][w:], y[1][w:]), z, 1)

    def leaf(self, c, live):
        @pl.when(~self.odd)
        def _():
            f = c // self.halves
            peer = self.place + 1
            self.up_copy(c, peer).wait_recv()
            top = self.top[c]
            weight = dot3(split(self.first[f]), split(top + self.urecv[c]), 0)
            if live is not None:
                weight = jnp.where(peer < live(f), weight, 0.0)
            self.top[c] = top - weight

            @pl.when(self.place % 4 == 0)
            def _():
                self.top_copy(c, self.place + 2).start()

            self.wsend[c] = weight
            self.back_copy(c, peer).start()

    def node(self, level, c, live):
        step = 1 << level

        @pl.when(self.place % (2 * step) == step)
        def _():
            f = c // self.halves
            self.lead_copy(c, self.place).wait_recv()
            if level > 1:
                self.rest_copy(c, self.place).wait_recv()
            rest = self.top[c] if level == 1 else self.rest_in[c]
            lead = self.lead_in[c]
            vectors = split(self.nvec[f, 0])
            inner = lead + dot3(vectors, split(rest), 0)
            weight = dot3(split(self.nfac[f, 0]), split(inner), 0)
            if live is not None:
                weight = jnp.where(self.place < live(f), weight, 0.0)
            self.hold[c] = lead - weight
            if 2 * step < self.blocks:
                @pl.when(self.place % (4 * step) == step)
                def _():
                    self.lead_copy(c, self.place + step).start()

                @pl.when(self.place % (4 * step) == 3 * step)
                def _():
                    self.rest_copy(c, self.place - step).start()
            else:
                self.at_root(c)
            self.fin[c] = rest - dot3(vectors, split(weight), 1)

    def climb(self, live):
        @pl.loop(0, self.chunks + self.levels - 1)
        def _(i):
            @pl.when(i < self.chunks)
            def _():
                self.leaf(i, live)

            for level in range(1, self.levels):
                @pl.when((i >= level) & (i < self.chunks + level))
                def _():
                    self.node(level, i - level, live)

    def finish(self, c, home_rows):
        f = c // self.halves

        @pl.when(self.place == 0)
        def _():
            self.home_copy(c, home_rows).wait_recv()
            self.fin[c, pl.ds(0, home_rows)] = self.rest_in[c, pl.ds(0, home_rows)]
            if home_rows < self.width:
                self.fin[c, pl.ds(home_rows, self.width - home_rows)] = jnp.zeros(
                    (self.width - home_rows, self.chunk), F32)

        @pl.when(self.odd)
        def _():
            self.back_copy(c, self.place).wait_recv()
            self.fin[c] = self.top[c] - dot3(split(self.nvec[f, 0]), split(self.wrecv[c]), 1)

    def result_copies(self, out, c):
        f, h = c // self.halves, c % self.halves
        columns = pl.ds(pl.multiple_of(h * self.chunk, self.chunk), self.chunk)
        w, rows = self.width, self.x.shape[1]
        return (
            pltpu.make_async_copy(self.body.at[c], out.at[f, pl.ds(w, rows - w), columns], self.fs.at[0, c]),
            pltpu.make_async_copy(self.fin.at[c], out.at[f, pl.ds(0, w), columns], self.fs.at[1, c]),
        )

    def drain(self, out, home_rows):
        root = self.blocks // 2

        @pl.when(self.odd)
        def _():
            for f in range(self.x.shape[0]):
                self.factor_copy(f, self.place).wait_send()

        @pl.loop(0, self.chunks)
        def _(c):
            @pl.when(self.odd)
            def _():
                self.up_copy(c, self.place).wait_send()

            @pl.when(~self.odd)
            def _():
                self.back_copy(c, self.place).wait_send()

            @pl.when(self.place % 4 == 0)
            def _():
                self.top_copy(c, self.place).wait_send()

            @pl.when((~self.odd) & (self.place != 0) & (self.place != root))
            def _():
                self.lead_copy(c, self.place).wait_send()

            @pl.when(self.place == root)
            def _():
                self.home_copy(c, home_rows).wait_send()

            for copy in self.result_copies(out, c):
                copy.wait()


def front_scratch(fronts, rows, cols, width, chunk):
    chunks = fronts * (cols // chunk)
    dma = pltpu.SemaphoreType.DMA
    piece = pltpu.VMEM((chunks, width, chunk), F32)
    return (
        [piece, pltpu.VMEM((chunks, rows - width, chunk), F32)]
        + [piece] * 8
        + [pltpu.VMEM((fronts, width, width), F32)]
        + [dma((chunks,))] * 8
        + [dma((fronts,))] * 2
        + [dma((2, chunks))]
    )


def kernel(blocks, columns, rows_ref, live_ref, lx, lv, lf, mv, mf, ux, uv, uf, sv, sf, out_low, out_up, *s):
    place, column = lax.axis_index("rows"), lax.axis_index("fronts")
    vlx, vlv, vlf, vmv, vmf, vux, vuv, vuf, vsv, vsf, portions, load_sem, part_s, part_r, over_s, over_r = s[:16]
    low = Front(blocks, vlx, vlv, vlf, vmv, vmf, mf, LOW_CHUNK, s[16:38])
    up = Front(blocks, vux, vuv, vuf, vsv, vsf, sf, UP_CHUNK, s[38:60])
    fronts = lx.shape[0]
    share = portions.shape[3]
    root = blocks // 2

    pairs = []
    for f in range(fronts):
        pairs += [(lx.at[f], vlx.at[f]), (lv.at[f], vlv.at[f]), (lf.at[f], vlf.at[f]), (mv.at[f], vmv.at[f])]
    first = len(pairs)
    pairs += [(mf, vmf), (ux, vux), (uv, vuv), (uf, vuf), (sv, vsv), (sf, vsf)]
    loads = [pltpu.make_async_copy(a, b, load_sem.at[i]) for i, (a, b) in enumerate(pairs)]
    for copy in loads:
        copy.start()

    barrier = pltpu.get_barrier_semaphore()
    for shift in range(1, blocks):
        pl.semaphore_signal(barrier, inc=1, device_id={"rows": (place + shift) % blocks},
                            device_id_type=pl.DeviceIdType.MESH)
    for shift in range(1, columns):
        pl.semaphore_signal(barrier, inc=1, device_id={"fronts": (column + shift) % columns},
                            device_id_type=pl.DeviceIdType.MESH)
    pl.semaphore_wait(barrier, blocks + columns - 2)
    low.send_factors()

    def live(f):
        return live_ref[column * fronts + f]

    for f in range(fronts):
        for copy in loads[4 * f:4 * f + 4]:
            copy.wait()

        @pl.loop(f * low.halves, (f + 1) * low.halves)
        def _(c):
            low.block(c, live)
            low.result_copies(out_low, c)[0].start()

    up.send_factors()
    for copy in loads[first:]:
        copy.wait()
    low.wait_factors()

    def part(c, r, peer):
        f, h = c // low.halves, c % low.halves
        return low.remote(
            low.hold.at[c, pl.ds(NPIV + r * share, share)], portions.at[column, f, h],
            part_s.at[r, c], part_r.at[c], peer)

    def over(c, shift, peer, slot):
        f, h = c // low.halves, c % low.halves
        return pltpu.make_async_remote_copy(
            portions.at[slot, f, h], portions.at[slot, f, h], over_s.at[shift, c], over_r.at[shift, c],
            device_id={"fronts": peer}, device_id_type=pl.DeviceIdType.MESH)

    def spread(c):
        for r in range(blocks):
            if r != root:
                part(c, r, r).start()
        portions[column, c // low.halves, c % low.halves] = low.hold[c, pl.ds(NPIV + root * share, share)]

    low.at_root = spread
    up.at_root = lambda c: up.home_copy(c, up.width).start()

    low.climb(live)

    @pl.loop(0, low.chunks)
    def _(c):
        @pl.when(place != root)
        def _():
            part(c, 0, place).wait_recv()

        for shift in range(1, columns):
            over(c, shift, (column + shift) % columns, column).start()

    @pl.when(place == root)
    def _():
        @pl.loop(0, low.chunks)
        def _(c):
            low.home_copy(c, NPIV).start()

    up.wait_factors()

    @pl.loop(0, low.chunks)
    def _(c):
        for shift in range(1, columns):
            over(c, shift, column, (column - shift + columns) % columns).wait_recv()

    height = vux.shape[1]
    here = rows_ref[...]
    hit = lax.broadcasted_iota(jnp.int32, (height, here.shape[1]), 0) == here
    chosen = jnp.where(hit, 1.0, 0.0)
    taken = jnp.sum(chosen, axis=1, keepdims=True) > 0.0
    chosen = chosen.astype(BF16)
    for h in range(low.halves):
        arrived = split(portions[:, :, h].reshape(here.shape[1], LOW_CHUNK))
        moved = jnp.dot(chosen, arrived[0], preferred_element_type=F32) + jnp.dot(
            chosen, arrived[1], preferred_element_type=F32)
        span = slice(h * LOW_CHUNK, (h + 1) * LOW_CHUNK)
        vux[0, :, span] = jnp.where(taken, moved, vux[0, :, span])

    @pl.loop(0, up.chunks)
    def _(c):
        up.block(c, None)
        up.result_copies(out_up, c)[0].start()

    up.climb(None)

    @pl.loop(0, low.chunks)
    def _(c):
        low.finish(c, NPIV)
        low.result_copies(out_low, c)[1].start()

    @pl.loop(0, up.chunks)
    def _(c):
        up.finish(c, up.width)
        up.result_copies(out_up, c)[1].start()

    @pl.when(place == root)
    def _():
        @pl.loop(0, low.chunks)
        def _(c):
            for r in range(blocks):
                if r != root:
                    part(c, r, r).wait_send()

    @pl.loop(0, low.chunks)
    def _(c):
        for shift in range(1, columns):
            over(c, shift, column, column).wait_send()

    low.drain(out_low, NPIV)
    up.drain(out_up, up.width)


def per_device(
    lower_rhs,
    lower_vectors,
    lower_factors,
    merge_vectors,
    merge_factors,
    live_blocks,
    parent_front,
    front_owner,
    contrib_rows,
    upper_rhs,
    upper_vectors,
    upper_factors,
    summit_vectors,
    summit_factors,
):
    place = lax.axis_index("rows")
    column = lax.axis_index("fronts")
    blocks = lax.axis_size("rows")
    columns = lax.axis_size("fronts")
    fronts, height, cols = lower_rhs.shape
    width = lower_factors.shape[-1]
    share = (width - NPIV) // blocks
    parents = jnp.arange(front_owner.shape[0], dtype=jnp.int32)
    target = jnp.sum(jnp.where(parent_front == parents[None, :], front_owner[None, :], 0), axis=1)
    rows_here = lax.dynamic_slice_in_dim(contrib_rows, place * share, share, 1) - place * height
    rows_here = jnp.where((target == column)[:, None], rows_here, -1).reshape(1, -1)
    dma = pltpu.SemaphoreType.DMA
    chunks = fronts * (cols // LOW_CHUNK)
    held = [lower_rhs, lower_vectors, lower_factors, merge_vectors, merge_factors]
    held += [upper_rhs, upper_vectors, upper_factors, summit_vectors, summit_factors]
    scratch = [pltpu.VMEM(a.shape, F32) for a in held]
    scratch += [
        pltpu.VMEM((columns, fronts, cols // LOW_CHUNK, share, LOW_CHUNK), F32),
        dma((4 * fronts + 6,)),
        dma((blocks, chunks)), dma((chunks,)), dma((columns, chunks)), dma((columns, chunks)),
    ]
    scratch += front_scratch(fronts, height, cols, width, LOW_CHUNK)
    scratch += front_scratch(upper_rhs.shape[0], height, cols, width, UP_CHUNK)
    anywhere = pl.BlockSpec(memory_space=pl.ANY)
    return pl.pallas_call(
        functools.partial(kernel, blocks, columns),
        out_shape=(
            jax.ShapeDtypeStruct(lower_rhs.shape, F32),
            jax.ShapeDtypeStruct(upper_rhs.shape, F32),
        ),
        in_specs=[pl.BlockSpec(memory_space=pltpu.VMEM), pl.BlockSpec(memory_space=pltpu.SMEM)] + [anywhere] * 10,
        out_specs=(anywhere, anywhere),
        scratch_shapes=scratch,
        compiler_params=pltpu.CompilerParams(
            collective_id=0, has_side_effects=True, vmem_limit_bytes=56 * 1024 * 1024),
        name="two_level",
    )(rows_here, live_blocks, lower_rhs, lower_vectors, lower_factors, merge_vectors, merge_factors,
      upper_rhs, upper_vectors, upper_factors, summit_vectors, summit_factors)


def solution(mesh):
    placed = (
        P("fronts", "rows", None),
        P("fronts", "rows", None),
        P("fronts", "rows", None, None),
        P("fronts", "rows", None, None),
        P("fronts", "rows", None, None),
        P(),
        P(),
        P(),
        P(),
        P("fronts", "rows", None),
        P("fronts", "rows", None),
        P("fronts", "rows", None, None),
        P("fronts", "rows", None, None),
        P("fronts", "rows", None, None),
    )
    return jax.shard_map(
        per_device,
        mesh=mesh,
        in_specs=placed,
        out_specs=(P("fronts", "rows", None), P("fronts", "rows", None)),
        check_vma=False,
    )
```

time: 185 us -> 107 us (0.58)
  Pallas kernels: 176 us -> 97.6 us
    pallas_call x1, Pallas kernels: 176 us -> 97.6 us  [per_device(): pl.pallas_call(functools.partial(kernel, blocks, columns), out_shape=(jax...]
where the time goes in v3:
time: 107 us
  Pallas kernels  97.6 us (91%)
  local copies, waits for them, and re-layouts  6.71 us (6%)
  other arithmetic  1.52 us (1%)
    pallas_call x1, Pallas kernels, per_device(): pl.pallas_call(functools.partial(kernel, blocks, columns), out_shape=(jax...  97.6 us
    unnamed x4, local copies, waits for them, and re-layouts  6.11 us

profile of v3, /device:TPU:0, one launch (start us, length us, event | category | flops | bytes accessed | tf_op | source)
XLA Modules:
  0.0 106.5 jit_solution(8663466326134338917)
XLA Ops:
  0.6 0.8 select_reduce_fusion
  1.4 0.8 subtract_select_fusion
  2.2 0.6 reshape.11.rows_ref
  2.8 97.6 %two_level.1 = (f32[2,1024,512]{2,1,0:T(8,128)}, f32[1,1024,512]{2,1,0:T(8,128)}) custom-call(s32[1,128]{1,0:T(1,128)} %reshape.11.rows_ref, s32[8]{0:T(128)} %live_ref.1, f32[2,1024,512]{2,1,0:T(8,128)} %lx.1, f32[2,1024,256]{2,1,0:T(8,128)} %lv.1, f32[2,1,256,256]{3,2,1,0:T(8,128)} %lf.1, f32[2,1,256,256]{3,2,1,0:T(8,128)} %mv.1, f32[2,1,256,256]{3,2,1,0:T(8,128)} %mf.1, ...), custom_call_target="tpu_custom_call" | custom-call | tf_op jit(solution)/shard_map/two_level/pallas_call | solution.py:411
  100.4 0.0 copy-start
  100.4 4.8 %copy.18 = f32[2,1024,512]{2,1,0:T(8,128)} copy(f32[2,1024,512]{2,1,0:T(8,128)} %get-tuple-element.4) | data formatting | bytes 8388608
  105.2 0.0 copy-done
  105.2 1.3 %copy.19 = f32[1,1024,512]{2,1,0:T(8,128)} copy(f32[1,1024,512]{2,1,0:T(8,128)S(1)} %copy-done) | data formatting | bytes 4194304
  (1 shorter events, 0.0 us)
Async XLA Ops:
  100.4 4.8 %copy-start = (f32[1,1024,512]{2,1,0:T(8,128)S(1)}, f32[1,1024,512]{2,1,0:T(8,128)}, u32[]{:S(2)}) copy-start(f32[1,1024,512]{2,1,0:T(8,128)} %get-tuple-element.5) | copy-start | bytes 6291460

commit v4 on v3

--- a/solution.py
+++ b/solution.py
@@ -31,11 +31,12 @@
         self.blocks, self.levels, self.chunk = blocks, blocks.bit_length() - 1, chunk
         self.x, self.vec, self.fac, self.nvec, self.nfac, self.nfac_any = x, vec, fac, nvec, nfac, nfac_any
         (self.top, self.body, self.usend, self.urecv, self.wsend, self.wrecv, self.fin, self.hold,
-         self.lead_in, self.rest_in, self.first,
+         self.lead_in, self.rest_in, self.scaled, self.first,
          self.us, self.ur, self.ws, self.wr, self.ts, self.hs, self.li, self.ri,
          self.gs, self.gr, self.fs) = s
         self.halves = x.shape[2] // chunk
-        self.chunks = x.shape[0] * self.halves
+        self.fronts = x.shape[0]
+        self.chunks = self.fronts * self.halves
         self.width = fac.shape[-1]
         self.place = lax.axis_index("rows")
         self.odd = self.place % 2 == 1
@@ -78,30 +79,41 @@
         span = pl.ds(0, rows)
         return self.remote(self.hold.at[c, span], self.rest_in.at[c, span], self.hs.at[c], self.ri.at[c], 0)
 
-    def block(self, c, live):
-        f, h = c // self.halves, c % self.halves
+    def tops(self, c, live, taken=None):
+        f, h = c % self.fronts, c // self.fronts
         columns = pl.ds(pl.multiple_of(h * self.chunk, self.chunk), self.chunk)
         x = self.x[f, :, columns]
+        if taken is not None:
+            x = jnp.where(taken, 0.0, x)
+            self.x[f, :, columns] = x
         y = split(self.vec[f])
         project = dot3(y, split(x), 0)
         scaled = dot3(split(self.fac[f, 0]), split(project), 0)
         if live is not None:
             scaled = jnp.where(self.place < live(f), scaled, 0.0)
-        z = split(scaled)
+        self.scaled[c] = scaled
         w = self.width
-        self.top[c] = x[:w] - dot3((y[0][:w], y[1][:w]), z, 1)
+        self.top[c] = x[:w] - dot3((y[0][:w], y[1][:w]), split(scaled), 1)
+
+    def send_up(self, c):
+        f = c % self.fronts
 
         @pl.when(self.odd)
         def _():
             self.usend[c] = dot3(split(self.nvec[f, 0]), split(self.top[c]), 0)
             self.up_copy(c, self.place - 1).start()
 
-        self.body[c] = x[w:] - dot3((y[0][w:], y[1][w:]), z, 1)
+    def bodies(self, c):
+        f, h = c % self.fronts, c // self.fronts
+        columns = pl.ds(pl.multiple_of(h * self.chunk, self.chunk), self.chunk)
+        w = self.width
+        lower = pl.ds(w, self.x.shape[1] - w)
+        self.body[c] = self.x[f, lower, columns] - dot3(split(self.vec[f, lower]), split(self.scaled[c]), 1)
 
     def leaf(self, c, live):
         @pl.when(~self.odd)
         def _():
-            f = c // self.halves
+            f = c % self.fronts
             peer = self.place + 1
             self.up_copy(c, peer).wait_recv()
             top = self.top[c]
@@ -122,7 +134,7 @@
 
         @pl.when(self.place % (2 * step) == step)
         def _():
-            f = c // self.halves
+            f = c % self.fronts
             self.lead_copy(c, self.place).wait_recv()
             if level > 1:
                 self.rest_copy(c, self.place).wait_recv()
@@ -159,7 +171,7 @@
                     self.node(level, i - level, live)
 
     def finish(self, c, home_rows):
-        f = c // self.halves
+        f = c % self.fronts
 
         @pl.when(self.place == 0)
         def _():
@@ -175,7 +187,7 @@
             self.fin[c] = self.top[c] - dot3(split(self.nvec[f, 0]), split(self.wrecv[c]), 1)
 
     def result_copies(self, out, c):
-        f, h = c // self.halves, c % self.halves
+        f, h = c % self.fronts, c // self.fronts
         columns = pl.ds(pl.multiple_of(h * self.chunk, self.chunk), self.chunk)
         w, rows = self.width, self.x.shape[1]
         return (
@@ -223,7 +235,7 @@
     piece = pltpu.VMEM((chunks, width, chunk), F32)
     return (
         [piece, pltpu.VMEM((chunks, rows - width, chunk), F32)]
-        + [piece] * 8
+        + [piece] * 9
         + [pltpu.VMEM((fronts, width, width), F32)]
         + [dma((chunks,))] * 8
         + [dma((fronts,))] * 2
@@ -231,11 +243,11 @@
     )
 
 
-def kernel(blocks, columns, rows_ref, live_ref, lx, lv, lf, mv, mf, ux, uv, uf, sv, sf, out_low, out_up, *s):
+def kernel(blocks, columns, rows_ref, live_ref, parent_ref, owner_ref, lx, lv, lf, mv, mf, ux, uv, uf, sv, sf, out_low, out_up, *s):
     place, column = lax.axis_index("rows"), lax.axis_index("fronts")
-    vlx, vlv, vlf, vmv, vmf, vux, vuv, vuf, vsv, vsf, portions, load_sem, part_s, part_r, over_s, over_r = s[:16]
-    low = Front(blocks, vlx, vlv, vlf, vmv, vmf, mf, LOW_CHUNK, s[16:38])
-    up = Front(blocks, vux, vuv, vuf, vsv, vsf, sf, UP_CHUNK, s[38:60])
+    vlx, vlv, vlf, vmv, vmf, vux, vuv, vuf, vsv, vsf, portions, tmat, load_sem, part_s, part_r, over_s, over_r = s[:17]
+    low = Front(blocks, vlx, vlv, vlf, vmv, vmf, mf, LOW_CHUNK, s[17:40])
+    up = Front(blocks, vux, vuv, vuf, vsv, vsf, sf, UP_CHUNK, s[40:63])
     fronts = lx.shape[0]
     share = portions.shape[3]
     root = blocks // 2
@@ -265,25 +277,65 @@
     for f in range(fronts):
         for copy in loads[4 * f:4 * f + 4]:
             copy.wait()
-
-        @pl.loop(f * low.halves, (f + 1) * low.halves)
-        def _(c):
-            low.block(c, live)
-            low.result_copies(out_low, c)[0].start()
+        low.tops(f, live)
+        low.send_up(f)
+
+    @pl.loop(fronts, low.chunks)
+    def _(c):
+        low.tops(c, live)
+        low.send_up(c)
 
     up.send_factors()
+
+    @pl.loop(0, low.chunks)
+    def _(c):
+        low.bodies(c)
+        low.result_copies(out_low, c)[0].start()
+
     for copy in loads[first:]:
         copy.wait()
+
+    height, total = vux.shape[1], rows_ref.shape[0]
+    lanes = rows_ref.shape[1]
+    spots = total * share
+    mine = jnp.broadcast_to(rows_ref[...].astype(F32)[:, None, :], (total, share, lanes)).reshape(spots, lanes)
+    spot = lax.broadcasted_iota(jnp.int32, (spots, lanes), 0)
+    lane = lax.broadcasted_iota(jnp.int32, (spots, lanes), 1)
+    child = spot // share
+    here_too = jnp.zeros((spots, lanes), F32)
+    for c in range(total):
+        owned = jnp.where(owner_ref[parent_ref[c, 0]] == column, 1.0, 0.0)
+        here_too = jnp.where(child == c, owned, here_too)
+    wanted = (lane == place * share + spot % share) & (here_too > 0.0)
+    base = (place * height).astype(F32)
+    offset = jnp.sum(jnp.where(wanted, mine - base + 1.0, 0.0), axis=1, keepdims=True) - 1.0
+    here = jnp.broadcast_to(offset, (spots, spots)).T[0:1]
+    hit = lax.broadcasted_iota(jnp.int32, (height, spots), 0).astype(F32) == here
+    chosen = jnp.where(hit, 1.0, 0.0)
+    taken = jnp.sum(chosen, axis=1, keepdims=True) > 0.0
+    y = split(vuv[0])
+    one = chosen.astype(BF16)
+    down = (((0,), (0,)), ((), ()))
+    gram = lax.dot_general(y[0], one, down, preferred_element_type=F32) + lax.dot_general(
+        y[1], one, down, preferred_element_type=F32)
+    inner = split(dot3(split(vuf[0, 0]), split(gram), 0))
+    tmat[...] = chosen - dot3(y, inner, 1)
+
+    @pl.loop(0, up.chunks)
+    def _(c):
+        up.tops(c, None, taken)
+        up.bodies(c)
+
     low.wait_factors()
 
     def part(c, r, peer):
-        f, h = c // low.halves, c % low.halves
+        f, h = c % fronts, c // fronts
         return low.remote(
             low.hold.at[c, pl.ds(NPIV + r * share, share)], portions.at[column, f, h],
             part_s.at[r, c], part_r.at[c], peer)
 
     def over(c, shift, peer, slot):
-        f, h = c // low.halves, c % low.halves
+        f, h = c % fronts, c // fronts
         return pltpu.make_async_remote_copy(
             portions.at[slot, f, h], portions.at[slot, f, h], over_s.at[shift, c], over_r.at[shift, c],
             device_id={"fronts": peer}, device_id_type=pl.DeviceIdType.MESH)
@@ -292,7 +344,7 @@
         for r in range(blocks):
             if r != root:
                 part(c, r, r).start()
-        portions[column, c // low.halves, c % low.halves] = low.hold[c, pl.ds(NPIV + root * share, share)]
+        portions[column, c % fronts, c // fronts] = low.hold[c, pl.ds(NPIV + root * share, share)]
 
     low.at_root = spread
     up.at_root = lambda c: up.home_copy(c, up.width).start()
@@ -314,31 +366,27 @@
         def _(c):
             low.home_copy(c, NPIV).start()
 
+    inside = LOW_CHUNK // UP_CHUNK
+
+    for h in range(low.halves):
+        for f in range(fronts):
+            for shift in range(1, columns):
+                over(h * fronts + f, shift, column, (column - shift + columns) % columns).wait_recv()
+        arrived = split(portions[:, :, h].reshape(spots, LOW_CHUNK))
+        gained = dot3(split(tmat[pl.ds(0, up.width)]), arrived, 1)
+        for k in range(inside):
+            c = h * inside + k
+            up.top[c] += gained[:, k * UP_CHUNK:(k + 1) * UP_CHUNK]
+            up.send_up(c)
+
+    @pl.loop(0, up.chunks)
+    def _(c):
+        h, k = c // inside, c % inside
+        arrived = split(portions[:, :, h, :, pl.ds(pl.multiple_of(k * UP_CHUNK, UP_CHUNK), UP_CHUNK)].reshape(spots, UP_CHUNK))
+        up.body[c] += dot3(split(tmat[pl.ds(up.width, height - up.width)]), arrived, 1)
+        up.result_copies(out_up, c)[0].start()
+
     up.wait_factors()
-
-    @pl.loop(0, low.chunks)
-    def _(c):
-        for shift in range(1, columns):
-            over(c, shift, column, (column - shift + columns) % columns).wait_recv()
-
-    height = vux.shape[1]
-    here = rows_ref[...]
-    hit = lax.broadcasted_iota(jnp.int32, (height, here.shape[1]), 0) == here
-    chosen = jnp.where(hit, 1.0, 0.0)
-    taken = jnp.sum(chosen, axis=1, keepdims=True) > 0.0
-    chosen = chosen.astype(BF16)
-    for h in range(low.halves):
-        arrived = split(portions[:, :, h].reshape(here.shape[1], LOW_CHUNK))
-        moved = jnp.dot(chosen, arrived[0], preferred_element_type=F32) + jnp.dot(
-            chosen, arrived[1], preferred_element_type=F32)
-        span = slice(h * LOW_CHUNK, (h + 1) * LOW_CHUNK)
-        vux[0, :, span] = jnp.where(taken, moved, vux[0, :, span])
-
-    @pl.loop(0, up.chunks)
-    def _(c):
-        up.block(c, None)
-        up.result_copies(out_up, c)[0].start()
-
     up.climb(None)
 
     @pl.loop(0, low.chunks)
@@ -384,17 +432,11 @@
     summit_vectors,
     summit_factors,
 ):
-    place = lax.axis_index("rows")
-    column = lax.axis_index("fronts")
     blocks = lax.axis_size("rows")
     columns = lax.axis_size("fronts")
     fronts, height, cols = lower_rhs.shape
     width = lower_factors.shape[-1]
     share = (width - NPIV) // blocks
-    parents = jnp.arange(front_owner.shape[0], dtype=jnp.int32)
-    target = jnp.sum(jnp.where(parent_front == parents[None, :], front_owner[None, :], 0), axis=1)
-    rows_here = lax.dynamic_slice_in_dim(contrib_rows, place * share, share, 1) - place * height
-    rows_here = jnp.where((target == column)[:, None], rows_here, -1).reshape(1, -1)
     dma = pltpu.SemaphoreType.DMA
     chunks = fronts * (cols // LOW_CHUNK)
     held = [lower_rhs, lower_vectors, lower_factors, merge_vectors, merge_factors]
@@ -402,6 +444,7 @@
     scratch = [pltpu.VMEM(a.shape, F32) for a in held]
     scratch += [
         pltpu.VMEM((columns, fronts, cols // LOW_CHUNK, share, LOW_CHUNK), F32),
+        pltpu.VMEM((height, contrib_rows.shape[0] * share), F32),
         dma((4 * fronts + 6,)),
         dma((blocks, chunks)), dma((chunks,)), dma((columns, chunks)), dma((columns, chunks)),
     ]
@@ -414,13 +457,13 @@
             jax.ShapeDtypeStruct(lower_rhs.shape, F32),
             jax.ShapeDtypeStruct(upper_rhs.shape, F32),
         ),
-        in_specs=[pl.BlockSpec(memory_space=pltpu.VMEM), pl.BlockSpec(memory_space=pltpu.SMEM)] + [anywhere] * 10,
+        in_specs=[pl.BlockSpec(memory_space=pltpu.VMEM)] + [pl.BlockSpec(memory_space=pltpu.SMEM)] * 3 + [anywhere] * 10,
         out_specs=(anywhere, anywhere),
         scratch_shapes=scratch,
         compiler_params=pltpu.CompilerParams(
             collective_id=0, has_side_effects=True, vmem_limit_bytes=56 * 1024 * 1024),
         name="two_level",
-    )(rows_here, live_blocks, lower_rhs, lower_vectors, lower_factors, merge_vectors, merge_factors,
+    )(contrib_rows, live_blocks, parent_front, front_owner, lower_rhs, lower_vectors, lower_factors, merge_vectors, merge_factors,
       upper_rhs, upper_vectors, upper_factors, summit_vectors, summit_factors)
 
 

time: 107 us -> 104 us (0.972)
  Pallas kernels: 97.6 us -> 95.4 us
  other arithmetic: 1.52 us -> 0 us
    pallas_call x1, Pallas kernels: 97.6 us -> 95.4 us  [per_device(): pl.pallas_call(functools.partial(kernel, blocks, columns), out_shape=(jax...]
    unnamed x4 -> x5, local copies, waits for them, and re-layouts: 6.11 us -> 7.43 us
where the time goes in v4:
time: 104 us; the launch traced here: 103 us
  Pallas kernels  95.4 us (92%)
  local copies, waits for them, and re-layouts  7.43 us (7%)
    pallas_call x1, Pallas kernels, per_device(): pl.pallas_call(functools.partial(kernel, blocks, columns), out_shape=(jax...  95.4 us
    unnamed x5, local copies, waits for them, and re-layouts  7.43 us

profile of v4, /device:TPU:0, one launch (start us, length us, event | category | flops | bytes accessed | tf_op | source)
XLA Modules:
  0.0 103.5 jit_solution(584829766006276310)
XLA Ops:
  0.6 1.3 %copy.16.parent_ref = s32[8,1]{1,0:T(8,128)} copy(s32[8,1]{0,1:T(1,128)} %param.20) | data formatting | bytes 64 | tf_op args[6]
  2.0 95.4 %two_level.1 = (f32[2,1024,512]{2,1,0:T(8,128)}, f32[1,1024,512]{2,1,0:T(8,128)}) custom-call(s32[8,128]{1,0:T(8,128)} %rows_ref.1, s32[8]{0:T(128)} %live_ref.1, s32[8,1]{1,0:T(8,128)} %copy.16.parent_ref, s32[4]{0:T(128)} %owner_ref.1, f32[2,1024,512]{2,1,0:T(8,128)} %lx.1, f32[2,1024,256]{2,1,0:T(8,128)} %lv.1, f32[2,1,256,256]{3,2,1,0:T(8,128)} %lf.1, ...), custom_call_target="tpu_custom_call" | custom-call | tf_op jit(solution)/shard_map/two_level/pallas_call | solution.py:454
  97.3 0.0 copy-start
  97.3 4.8 %copy.19 = f32[2,1024,512]{2,1,0:T(8,128)} copy(f32[2,1024,512]{2,1,0:T(8,128)} %get-tuple-element.4) | data formatting | bytes 8388608
  102.1 0.0 copy-done
  102.1 1.3 %copy.20 = f32[1,1024,512]{2,1,0:T(8,128)} copy(f32[1,1024,512]{2,1,0:T(8,128)S(1)} %copy-done) | data formatting | bytes 4194304
Async XLA Ops:
  97.3 4.8 %copy-start = (f32[1,1024,512]{2,1,0:T(8,128)S(1)}, f32[1,1024,512]{2,1,0:T(8,128)}, u32[]{:S(2)}) copy-start(f32[1,1024,512]{2,1,0:T(8,128)} %get-tuple-element.5) | copy-start | bytes 6291460

commit v5 on v4

--- a/solution.py
+++ b/solution.py
@@ -19,10 +19,13 @@
     return high, (x - high.astype(F32)).astype(BF16)
 
 
-def dot3(a, b, side):
+def pair(ref, f):
+    return ref[0, f], ref[1, f]
+
+
+def dot3(a, b):
     (ah, al), (bh, bl) = a, b
-    dims = (((side,), (0,)), ((), ()))
-    one = functools.partial(lax.dot_general, dimension_numbers=dims, preferred_element_type=F32)
+    one = functools.partial(jnp.dot, preferred_element_type=F32)
     return one(ah, bh) + (one(ah, bl) + one(al, bh))
 
 
@@ -32,6 +35,7 @@
         self.x, self.vec, self.fac, self.nvec, self.nfac, self.nfac_any = x, vec, fac, nvec, nfac, nfac_any
         (self.top, self.body, self.usend, self.urecv, self.wsend, self.wrecv, self.fin, self.hold,
          self.lead_in, self.rest_in, self.scaled, self.first,
+         self.yt, self.vt, self.gt, self.ft, self.first_t,
          self.us, self.ur, self.ws, self.wr, self.ts, self.hs, self.li, self.ri,
          self.gs, self.gr, self.fs) = s
         self.halves = x.shape[2] // chunk
@@ -59,6 +63,19 @@
         def _():
             for f in range(self.x.shape[0]):
                 self.factor_copy(f, self.place).wait_recv()
+                self.keep(self.first_t, f, self.first[f])
+
+    def keep(self, ref, f, value):
+        ref[0, f], ref[1, f] = split(value.T)
+
+    def turn(self, f):
+        self.keep(self.yt, f, self.vec[f])
+        self.keep(self.ft, f, self.fac[f, 0])
+        self.keep(self.vt, f, self.nvec[f, 0])
+
+    def turn_nodes(self):
+        for f in range(self.x.shape[0]):
+            self.keep(self.gt, f, self.nfac[f, 0])
 
     def up_copy(self, c, peer):
         return self.remote(self.usend.at[c], self.urecv.at[c], self.us.at[c], self.ur.at[c], peer)
@@ -79,28 +96,24 @@
         span = pl.ds(0, rows)
         return self.remote(self.hold.at[c, span], self.rest_in.at[c, span], self.hs.at[c], self.ri.at[c], 0)
 
-    def tops(self, c, live, taken=None):
+    def tops(self, c, live):
         f, h = c % self.fronts, c // self.fronts
         columns = pl.ds(pl.multiple_of(h * self.chunk, self.chunk), self.chunk)
         x = self.x[f, :, columns]
-        if taken is not None:
-            x = jnp.where(taken, 0.0, x)
-            self.x[f, :, columns] = x
-        y = split(self.vec[f])
-        project = dot3(y, split(x), 0)
-        scaled = dot3(split(self.fac[f, 0]), split(project), 0)
+        project = dot3(pair(self.yt, f), split(x))
+        scaled = dot3(pair(self.ft, f), split(project))
         if live is not None:
             scaled = jnp.where(self.place < live(f), scaled, 0.0)
         self.scaled[c] = scaled
         w = self.width
-        self.top[c] = x[:w] - dot3((y[0][:w], y[1][:w]), split(scaled), 1)
+        self.top[c] = x[:w] - dot3(split(self.vec[f, pl.ds(0, w)]), split(scaled))
 
     def send_up(self, c):
         f = c % self.fronts
 
         @pl.when(self.odd)
         def _():
-            self.usend[c] = dot3(split(self.nvec[f, 0]), split(self.top[c]), 0)
+            self.usend[c] = dot3(pair(self.vt, f), split(self.top[c]))
             self.up_copy(c, self.place - 1).start()
 
     def bodies(self, c):
@@ -108,7 +121,7 @@
         columns = pl.ds(pl.multiple_of(h * self.chunk, self.chunk), self.chunk)
         w = self.width
         lower = pl.ds(w, self.x.shape[1] - w)
-        self.body[c] = self.x[f, lower, columns] - dot3(split(self.vec[f, lower]), split(self.scaled[c]), 1)
+        self.body[c] = self.x[f, lower, columns] - dot3(split(self.vec[f, lower]), split(self.scaled[c]))
 
     def leaf(self, c, live):
         @pl.when(~self.odd)
@@ -117,7 +130,7 @@
             peer = self.place + 1
             self.up_copy(c, peer).wait_recv()
             top = self.top[c]
-            weight = dot3(split(self.first[f]), split(top + self.urecv[c]), 0)
+            weight = dot3(pair(self.first_t, f), split(top + self.urecv[c]))
             if live is not None:
                 weight = jnp.where(peer < live(f), weight, 0.0)
             self.top[c] = top - weight
@@ -140,9 +153,8 @@
                 self.rest_copy(c, self.place).wait_recv()
             rest = self.top[c] if level == 1 else self.rest_in[c]
             lead = self.lead_in[c]
-            vectors = split(self.nvec[f, 0])
-            inner = lead + dot3(vectors, split(rest), 0)
-            weight = dot3(split(self.nfac[f, 0]), split(inner), 0)
+            inner = lead + dot3(pair(self.vt, f), split(rest))
+            weight = dot3(pair(self.gt, f), split(inner))
             if live is not None:
                 weight = jnp.where(self.place < live(f), weight, 0.0)
             self.hold[c] = lead - weight
@@ -156,10 +168,10 @@
                     self.rest_copy(c, self.place - step).start()
             else:
                 self.at_root(c)
-            self.fin[c] = rest - dot3(vectors, split(weight), 1)
-
-    def climb(self, live):
-        @pl.loop(0, self.chunks + self.levels - 1)
+            self.fin[c] = rest - dot3(split(self.nvec[f, 0]), split(weight))
+
+    def climb(self, live, ahead=None, units=0):
+        @pl.loop(0, max(self.chunks + self.levels - 1, units))
         def _(i):
             @pl.when(i < self.chunks)
             def _():
@@ -169,6 +181,11 @@
                 @pl.when((i >= level) & (i < self.chunks + level))
                 def _():
                     self.node(level, i - level, live)
+
+            if ahead is not None:
+                @pl.when(i < units)
+                def _():
+                    ahead(i)
 
     def finish(self, c, home_rows):
         f = c % self.fronts
@@ -184,7 +201,7 @@
         @pl.when(self.odd)
         def _():
             self.back_copy(c, self.place).wait_recv()
-            self.fin[c] = self.top[c] - dot3(split(self.nvec[f, 0]), split(self.wrecv[c]), 1)
+            self.fin[c] = self.top[c] - dot3(split(self.nvec[f, 0]), split(self.wrecv[c]))
 
     def result_copies(self, out, c):
         f, h = c % self.fronts, c // self.fronts
@@ -236,7 +253,8 @@
     return (
         [piece, pltpu.VMEM((chunks, rows - width, chunk), F32)]
         + [piece] * 9
-        + [pltpu.VMEM((fronts, width, width), F32)]
+        + [pltpu.VMEM((fronts, width, width), F32), pltpu.VMEM((2, fronts, width, rows), BF16)]
+        + [pltpu.VMEM((2, fronts, width, width), BF16)] * 4
         + [dma((chunks,))] * 8
         + [dma((fronts,))] * 2
         + [dma((2, chunks))]
@@ -246,8 +264,8 @@
 def kernel(blocks, columns, rows_ref, live_ref, parent_ref, owner_ref, lx, lv, lf, mv, mf, ux, uv, uf, sv, sf, out_low, out_up, *s):
     place, column = lax.axis_index("rows"), lax.axis_index("fronts")
     vlx, vlv, vlf, vmv, vmf, vux, vuv, vuf, vsv, vsf, portions, tmat, load_sem, part_s, part_r, over_s, over_r = s[:17]
-    low = Front(blocks, vlx, vlv, vlf, vmv, vmf, mf, LOW_CHUNK, s[17:40])
-    up = Front(blocks, vux, vuv, vuf, vsv, vsf, sf, UP_CHUNK, s[40:63])
+    low = Front(blocks, vlx, vlv, vlf, vmv, vmf, mf, LOW_CHUNK, s[17:45])
+    up = Front(blocks, vux, vuv, vuf, vsv, vsf, sf, UP_CHUNK, s[45:73])
     fronts = lx.shape[0]
     share = portions.shape[3]
     root = blocks // 2
@@ -277,6 +295,7 @@
     for f in range(fronts):
         for copy in loads[4 * f:4 * f + 4]:
             copy.wait()
+        low.turn(f)
         low.tops(f, live)
         low.send_up(f)
 
@@ -294,6 +313,7 @@
 
     for copy in loads[first:]:
         copy.wait()
+    low.turn_nodes()
 
     height, total = vux.shape[1], rows_ref.shape[0]
     lanes = rows_ref.shape[1]
@@ -304,7 +324,7 @@
     child = spot // share
     here_too = jnp.zeros((spots, lanes), F32)
     for c in range(total):
-        owned = jnp.where(owner_ref[parent_ref[c, 0]] == column, 1.0, 0.0)
+        owned = jnp.where(owner_ref[parent_ref[c]] == column, 1.0, 0.0)
         here_too = jnp.where(child == c, owned, here_too)
     wanted = (lane == place * share + spot % share) & (here_too > 0.0)
     base = (place * height).astype(F32)
@@ -313,17 +333,17 @@
     hit = lax.broadcasted_iota(jnp.int32, (height, spots), 0).astype(F32) == here
     chosen = jnp.where(hit, 1.0, 0.0)
     taken = jnp.sum(chosen, axis=1, keepdims=True) > 0.0
-    y = split(vuv[0])
+    up.turn(0)
+    up.turn_nodes()
     one = chosen.astype(BF16)
-    down = (((0,), (0,)), ((), ()))
-    gram = lax.dot_general(y[0], one, down, preferred_element_type=F32) + lax.dot_general(
-        y[1], one, down, preferred_element_type=F32)
-    inner = split(dot3(split(vuf[0, 0]), split(gram), 0))
-    tmat[...] = chosen - dot3(y, inner, 1)
-
-    @pl.loop(0, up.chunks)
-    def _(c):
-        up.tops(c, None, taken)
+    gram = jnp.dot(up.yt[0, 0], one, preferred_element_type=F32) + jnp.dot(
+        up.yt[1, 0], one, preferred_element_type=F32)
+    inner = split(dot3(pair(up.ft, 0), split(gram)))
+    tmat[...] = chosen - dot3(split(vuv[0]), inner)
+    vux[0] = jnp.where(taken, 0.0, vux[0])
+
+    def ahead(c):
+        up.tops(c, None)
         up.bodies(c)
 
     low.wait_factors()
@@ -349,7 +369,7 @@
     low.at_root = spread
     up.at_root = lambda c: up.home_copy(c, up.width).start()
 
-    low.climb(live)
+    low.climb(live, ahead, up.chunks)
 
     @pl.loop(0, low.chunks)
     def _(c):
@@ -366,6 +386,7 @@
         def _(c):
             low.home_copy(c, NPIV).start()
 
+    up.wait_factors()
     inside = LOW_CHUNK // UP_CHUNK
 
     for h in range(low.halves):
@@ -373,7 +394,7 @@
             for shift in range(1, columns):
                 over(h * fronts + f, shift, column, (column - shift + columns) % columns).wait_recv()
         arrived = split(portions[:, :, h].reshape(spots, LOW_CHUNK))
-        gained = dot3(split(tmat[pl.ds(0, up.width)]), arrived, 1)
+        gained = dot3(split(tmat[pl.ds(0, up.width)]), arrived)
         for k in range(inside):
             c = h * inside + k
             up.top[c] += gained[:, k * UP_CHUNK:(k + 1) * UP_CHUNK]
@@ -383,10 +404,9 @@
     def _(c):
         h, k = c // inside, c % inside
         arrived = split(portions[:, :, h, :, pl.ds(pl.multiple_of(k * UP_CHUNK, UP_CHUNK), UP_CHUNK)].reshape(spots, UP_CHUNK))
-        up.body[c] += dot3(split(tmat[pl.ds(up.width, height - up.width)]), arrived, 1)
+        up.body[c] += dot3(split(tmat[pl.ds(up.width, height - up.width)]), arrived)
         up.result_copies(out_up, c)[0].start()
 
-    up.wait_factors()
     up.climb(None)
 
     @pl.loop(0, low.chunks)
@@ -463,7 +483,7 @@
         compiler_params=pltpu.CompilerParams(
             collective_id=0, has_side_effects=True, vmem_limit_bytes=56 * 1024 * 1024),
         name="two_level",
-    )(contrib_rows, live_blocks, parent_front, front_owner, lower_rhs, lower_vectors, lower_factors, merge_vectors, merge_factors,
+    )(contrib_rows, live_blocks, parent_front.reshape(-1), front_owner, lower_rhs, lower_vectors, lower_factors, merge_vectors, merge_factors,
       upper_rhs, upper_vectors, upper_factors, summit_vectors, summit_factors)
 
 

time: 104 us -> 101 us (0.971)
  local copies, waits for them, and re-layouts: 7.43 us -> 6.11 us
    unnamed x5 -> x4, local copies, waits for them, and re-layouts: 7.43 us -> 6.11 us
where the time goes in v5:
time: 101 us
  Pallas kernels  94.5 us (94%)
  local copies, waits for them, and re-layouts  6.11 us (6%)
    pallas_call x1, Pallas kernels, per_device(): pl.pallas_call(functools.partial(kernel, blocks, columns), out_shape=(jax...  94.5 us
    unnamed x4, local copies, waits for them, and re-layouts  6.11 us

profile of v5, /device:TPU:0, one launch (start us, length us, event | category | flops | bytes accessed | tf_op | source)
XLA Modules:
  0.0 101.2 jit_solution(2412763137132557751)
XLA Ops:
  0.6 94.5 %two_level.1 = (f32[2,1024,512]{2,1,0:T(8,128)}, f32[1,1024,512]{2,1,0:T(8,128)}) custom-call(s32[8,128]{1,0:T(8,128)} %rows_ref.1, s32[8]{0:T(128)} %live_ref.1, s32[8]{0:T(128)} %bitcast.1, s32[4]{0:T(128)} %owner_ref.1, f32[2,1024,512]{2,1,0:T(8,128)} %lx.1, f32[2,1024,256]{2,1,0:T(8,128)} %lv.1, f32[2,1,256,256]{3,2,1,0:T(8,128)} %lf.1, ...), custom_call_target="tpu_custom_call" | custom-call | tf_op jit(solution)/shard_map/two_level/pallas_call | solution.py:474
  95.1 0.0 copy-start
  95.1 4.8 %copy.18 = f32[2,1024,512]{2,1,0:T(8,128)} copy(f32[2,1024,512]{2,1,0:T(8,128)} %get-tuple-element.4) | data formatting | bytes 8388608
  99.9 0.0 copy-done
  99.9 1.3 %copy.19 = f32[1,1024,512]{2,1,0:T(8,128)} copy(f32[1,1024,512]{2,1,0:T(8,128)S(1)} %copy-done) | data formatting | bytes 4194304
Async XLA Ops:
  95.1 4.8 %copy-start = (f32[1,1024,512]{2,1,0:T(8,128)S(1)}, f32[1,1024,512]{2,1,0:T(8,128)}, u32[]{:S(2)}) copy-start(f32[1,1024,512]{2,1,0:T(8,128)} %get-tuple-element.5) | copy-start | bytes 6291460

commit v6 on v5

--- a/solution.py
+++ b/solution.py
@@ -8,7 +8,7 @@
 from jax.sharding import PartitionSpec as P
 
 NPIV = 128
-LOW_CHUNK = 256
+LOW_CHUNK = 128
 UP_CHUNK = 128
 F32 = jnp.float32
 BF16 = jnp.bfloat16

time: 101 us -> 104 us (1.030)
  Pallas kernels: 94.5 us -> 97.5 us
    pallas_call x1, Pallas kernels: 94.5 us -> 97.5 us  [per_device(): pl.pallas_call(functools.partial(kernel, blocks, columns), out_shape=(jax...]
where the time goes in v6:
time: 104 us
  Pallas kernels  97.5 us (94%)
  local copies, waits for them, and re-layouts  6.11 us (6%)
    pallas_call x1, Pallas kernels, per_device(): pl.pallas_call(functools.partial(kernel, blocks, columns), out_shape=(jax...  97.5 us
    unnamed x4, local copies, waits for them, and re-layouts  6.11 us

profile of v6, /device:TPU:0, one launch (start us, length us, event | category | flops | bytes accessed | tf_op | source)
XLA Modules:
  0.0 104.3 jit_solution(13683367077705059558)
XLA Ops:
  0.6 97.5 %two_level.1 = (f32[2,1024,512]{2,1,0:T(8,128)}, f32[1,1024,512]{2,1,0:T(8,128)}) custom-call(s32[8,128]{1,0:T(8,128)} %rows_ref.1, s32[8]{0:T(128)} %live_ref.1, s32[8]{0:T(128)} %bitcast.1, s32[4]{0:T(128)} %owner_ref.1, f32[2,1024,512]{2,1,0:T(8,128)} %lx.1, f32[2,1024,256]{2,1,0:T(8,128)} %lv.1, f32[2,1,256,256]{3,2,1,0:T(8,128)} %lf.1, ...), custom_call_target="tpu_custom_call" | custom-call | tf_op jit(solution)/shard_map/two_level/pallas_call | solution.py:474
  98.2 0.0 copy-start
  98.2 4.8 %copy.18 = f32[2,1024,512]{2,1,0:T(8,128)} copy(f32[2,1024,512]{2,1,0:T(8,128)} %get-tuple-element.4) | data formatting | bytes 8388608
  103.0 0.0 copy-done
  103.0 1.3 %copy.19 = f32[1,1024,512]{2,1,0:T(8,128)} copy(f32[1,1024,512]{2,1,0:T(8,128)S(1)} %copy-done) | data formatting | bytes 4194304
Async XLA Ops:
  98.2 4.8 %copy-start = (f32[1,1024,512]{2,1,0:T(8,128)S(1)}, f32[1,1024,512]{2,1,0:T(8,128)}, u32[]{:S(2)}) copy-start(f32[1,1024,512]{2,1,0:T(8,128)} %get-tuple-element.5) | copy-start | bytes 6291460
